TPU v7x, 128 devices: a whole 4x4x4 slice. The times are simulated.
128 devices in a mesh: shard: 4 (over y_lo, core), context: 8 (over y_hi, z), tensor: 4 (over x).
Axes of the slice: x: 4, y: 4 (y_hi: 2, y_lo: 2; y = y_hi * 2 + y_lo), z: 4, core: 2. Of those that a mesh axis runs over, the one named last changes fastest.
Arguments:
- inputs: bfloat16 [16, 1024, 2048], P('shard', 'context'), may hold values from -6 to 6
- cotangent: bfloat16 [16, 1024, 2048], P('shard', 'context'), may hold values from -6 to 6
- q_weight: bfloat16 [2048, 2048], P('shard', 'tensor'), may hold values from -0.125 to 0.125
- k_weight: bfloat16 [2048, 2048], P('shard', 'tensor'), may hold values from -0.125 to 0.125
- v_weight: bfloat16 [2048, 2048], P('shard', 'tensor'), may hold values from -0.125 to 0.125
- o_weight: bfloat16 [2048, 2048], P('tensor', 'shard'), may hold values from -2 to 2
- gate_weight: bfloat16 [2048, 8192], P('shard', 'tensor'), may hold values from -0.125 to 0.125
- up_weight: bfloat16 [2048, 8192], P('shard', 'tensor'), may hold values from -0.125 to 0.125
- down_weight: bfloat16 [8192, 2048], P('tensor', 'shard'), may hold values from -0.125 to 0.125
- attn_gain: bfloat16 [2048], P('shard'), may hold values from 0.099609375 to 1.8984375
- ffn_gain: bfloat16 [2048], P('shard'), may hold values from 0.099609375 to 1.8984375
- piece_starts: int32 [16, 2], P('shard'), may hold values from 0 to 768, as said below
- piece_ids: int32 [16, 2], P('shard'), may hold values from 0 to 1
- valid_mask: int32 [16, 1024], P('shard'), may hold values from 0 to 1, as said below
Outputs:
- output: bfloat16 [16, 1024, 2048], P('shard', 'context')
- input_grad: bfloat16 [16, 1024, 2048], P('shard', 'context')
- q_grad: float32 [2048, 2048], P('shard', 'tensor')
- k_grad: float32 [2048, 2048], P('shard', 'tensor')
- v_grad: float32 [2048, 2048], P('shard', 'tensor')
- o_grad: float32 [2048, 2048], P('tensor', 'shard')
- gate_grad: float32 [2048, 8192], P('shard', 'tensor')
- up_grad: float32 [2048, 8192], P('shard', 'tensor')
- down_grad: float32 [8192, 2048], P('tensor', 'shard')
- attn_gain_grad: float32 [2048], P(('shard', 'tensor'))
- ffn_gain_grad: float32 [2048], P(('shard', 'tensor'))
- branch_rms: float32 [3], replicated
Inputs may be any that keep to these rules, and one draw needn't show every extreme that they name: `piece_starts`: the 2 pieces of a sequence do not intersection: piece p starts between p * 512 and (p + 1) * 512 - 256. `piece_ids`: pieces of one sequence with equal ids show one picture. `valid_mask`: the real tokens of a sequence are a prefix of 256 to 1024 tokens; both lengths occur in every draw.
All inputs are finite; a program needn't handle non-finite values.
Results may differ from a plain program's by a relative error of at most 0.03.
Values may be sent and summed in bfloat16 or wider, within the bound.
A program may use at most 256 MiB of HBM per device.

v0:
```python
import functools

import jax
import jax.numpy as jnp
import numpy as np
from jax import lax
from jax.experimental import pallas as pl
from jax.experimental.pallas import tpu as pltpu
from jax.sharding import PartitionSpec as P

HEAD_DIM = 64
PIECE = 256
NORM_EPS = 1e-05
ROPE_BASE = 130000.0
MASK_FILL = -1e30
BF = jnp.bfloat16
F32 = jnp.float32
ANY = pl.BlockSpec(memory_space=pl.ANY)
VM = pl.BlockSpec(memory_space=pltpu.VMEM)
DMA = pltpu.SemaphoreType.DMA
PROJ_ORDER = "gxxxxxggxgxgxgxggx"
MID_ORDER = "amcmmammbacmcdbambmdcmbmdxacxxbdmxamdxbmdxcmmxcdbaxdbcaxmbammmxx"
ATTEND_ROWS = 256
LAST_ORDER = "bxaxdbxxbxabaxcdxbcdxacsbadsbxsaxdadccaabdcbscddscc"
FFN_TILE, FFN_ROWS, FFN_BACK = 256, 1024, 2048
VMEM_LIMIT = 60 * 1024 * 1024
MODEL = 2048
TILE = 256
BLOCK = 128
MESH_ID = pl.DeviceIdType.MESH


class Place:
    def __init__(self):
        self.s = lax.axis_index("shard")
        self.k = lax.axis_index("context")
        self.x = lax.axis_index("tensor")
        self.yl = self.s // 2
        self.c = self.s % 2
        self.y = (self.k // 4) * 2 + self.yl
        self.z = self.k % 4

    def dev(self, dx=0, dy=0, dz=0, core=None):
        x = (self.x + dx + 4) % 4
        y = (self.y + dy + 4) % 4
        z = (self.z + dz + 4) % 4
        c = self.c if core is None else core
        return {"shard": (y % 2) * 2 + c, "context": (y // 2) * 4 + z, "tensor": x}

    def member(self, k):
        return {"shard": self.s, "context": k, "tensor": self.x}

    def slot(self, k):
        return (k // 2) * 2 + (k % 2 + self.c) % 2

    def sib(self):
        return self.dev(core=1 - self.c)


def remote(src, dst, send_sem, recv_sem, device):
    return pltpu.make_async_remote_copy(
        src_ref=src,
        dst_ref=dst,
        send_sem=send_sem,
        recv_sem=recv_sem,
        device_id=device,
        device_id_type=MESH_ID,
    )


def greet(devices):
    barrier = pltpu.get_barrier_semaphore()
    for d in devices:
        pl.semaphore_signal(barrier, inc=1, device_id=d, device_id_type=MESH_ID)
    pl.semaphore_wait(barrier, len(devices))


def params(collective_id=None):
    if collective_id is None:
        return pltpu.CompilerParams(vmem_limit_bytes=VMEM_LIMIT)
    return pltpu.CompilerParams(
        vmem_limit_bytes=VMEM_LIMIT, collective_id=collective_id, has_side_effects=True
    )


def tiles(v):
    return v.reshape(*v.shape[:-2], v.shape[-2] // 8, 8, v.shape[-1])


def rows_of(v):
    return v.reshape(*v.shape[:-3], v.shape[-3] * 8, v.shape[-1])


def context_peers(p):
    return [p.member((p.k + d) % 8) for d in range(1, 8)]


def swap_halves(v):
    width = v.shape[1]
    lane = lax.broadcasted_iota(jnp.int32, v.shape, 1) % HEAD_DIM
    return jnp.where(
        lane < HEAD_DIM // 2,
        pltpu.roll(v, width - HEAD_DIM // 2, 1),
        pltpu.roll(v, HEAD_DIM // 2, 1),
    )


WEIGHTS = (
    (256, "row", 0),
    (256, "row", 256),
    (256, "row", 512),
    (256, "col", 0),
    (1024, "row", 0),
    (1024, "row", 1024),
    (1024, "col", 0),
)


class Gather:
    def __init__(self, p, ws, srcs, dsts, stages, sems):
        self.p, self.ws, self.srcs, self.dsts, self.stages = p, ws, srcs, dsts, stages
        self.y_send, self.y_recv, self.z_send, self.z_recv, self.s_send, self.s_recv, self.loc = sems
        self.qa = 2 * (p.z % 2)

    @staticmethod
    def sems(n):
        return [DMA((n, 2, 2))] * 4 + [DMA((n,))] * 3

    @staticmethod
    def peers(p):
        return (
            [p.sib()]
            + [p.dev(dy=dy, core=core) for dy in (-1, 1) for core in (0, 1)]
            + [p.dev(dz=1), p.dev(dz=-1)]
        )

    def src(self, i, half, quarter):
        size, kind, _ = WEIGHTS[self.ws[i]]
        if kind == "row":
            rows = pl.ds(0, 64) if quarter is None else pl.ds(quarter * 16, 16)
            return self.srcs[i].at[rows, :, pl.ds(half * size, size)]
        size = size // 8
        if quarter is None:
            return self.srcs[i].at[pl.ds(half * size, size)]
        return self.srcs[i].at[pl.ds(half * size + quarter * (size // 4), size // 4)]

    def dst(self, i, block, quarter):
        size, kind, off = WEIGHTS[self.ws[i]]
        if kind == "row":
            rows = (
                pl.ds(block * 64, 64)
                if quarter is None
                else pl.ds(block * 64 + quarter * 16, 16)
            )
            return self.dsts[i].at[rows, :, pl.ds(off, size)]
        size = size // 8
        cols = pl.ds(block * 512, 512)
        if quarter is None:
            return self.dsts[i].at[:, :, cols]
        return self.dsts[i].at[pl.ds(quarter * (size // 4), size // 4), :, cols]

    def y_copy(self, i, side, core):
        p = self.p
        quarter = self.qa + side
        return remote(
            self.src(i, core, quarter),
            self.dst(i, p.s, quarter),
            self.y_send.at[i, side, core],
            self.y_recv.at[i, side, p.c],
            p.dev(dy=-1 if side == 0 else 1, core=core),
        )

    def y_arrival(self, i, side, core):
        p = self.p
        here = self.dst(i, (1 - p.yl) * 2 + core, self.qa + side)
        return remote(
            here,
            here,
            self.y_send.at[i, side, core],
            self.y_recv.at[i, side, core],
            p.dev(dy=1 if side == 0 else -1, core=core),
        )

    def z_copy(self, i, side, core, arrival=False):
        p = self.p
        quarter = 2 - self.qa + side if arrival else self.qa + side
        here = self.dst(i, (1 - p.yl) * 2 + core, quarter)
        return remote(
            here,
            here,
            self.z_send.at[i, side, core],
            self.z_recv.at[i, side, core],
            p.dev(dz=1 if (side == 0) == arrival else -1),
        )

    def sib_copy(self, i, arrival=False):
        p = self.p
        there = self.dst(i, p.yl * 2 + 1 - p.c if arrival else p.s, None)
        return remote(
            there if arrival else self.src(i, 1 - p.c, None),
            there,
            self.s_send.at[i],
            self.s_recv.at[i],
            p.sib(),
        )

    def own_copy(self, i, step):
        stage = self.stages[i]
        here = self.dst(i, self.p.s, None)
        if step == 1:
            return pltpu.make_async_copy(stage, here, self.loc.at[i])
        return pltpu.make_async_copy(
            self.src(i, self.p.c, None), here if stage is None else stage, self.loc.at[i]
        )

    def start(self):
        for i in range(len(self.ws)):
            for core in (0, 1):
                for side in (0, 1):
                    self.y_copy(i, side, core).start()
        for i in range(len(self.ws)):
            self.sib_copy(i).start()
            self.own_copy(i, 0).start()

    def pass_on(self, i):
        for side in (0, 1):
            for core in (0, 1):
                self.y_arrival(i, side, core).wait_recv()
                self.z_copy(i, side, core).start()
        if self.stages[i] is not None:
            self.own_copy(i, 0).wait()
            self.own_copy(i, 1).start()

    def arrive(self, i):
        for side in (0, 1):
            for core in (0, 1):
                self.z_copy(i, side, core, True).wait_recv()
        self.sib_copy(i, True).wait_recv()
        self.own_copy(i, 0 if self.stages[i] is None else 1).wait()

    def sent(self, i):
        self.sib_copy(i).wait_send()
        for side in (0, 1):
            for core in (0, 1):
                self.y_copy(i, side, core).wait_send()
                self.z_copy(i, side, core).wait_send()

    def steps(self):
        self.start()
        yield
        for i in range(len(self.ws)):
            self.pass_on(i)
            yield
        for i in range(len(self.ws)):
            self.arrive(i)
            self.sent(i)
            yield


def run(order, **gens):
    alive = dict(gens)

    def step(name):
        if name in alive:
            try:
                next(alive[name])
            except StopIteration:
                del alive[name]

    for name in order:
        step(name)
    while alive:
        for name in list(alive):
            step(name)


def start_kernel(
    x_ref,
    cot_ref,
    wq,
    wk,
    wv,
    wo,
    gain_ref,
    meta_ref,
    rope_ref,
    wqkv_o,
    wo_o,
    gains_o,
    meta_o,
    cot_o,
    attn_in_t_o,
    qkv_o,
    attn_in,
    x_all,
    qkv_send,
    stage_o,
    stage_cot,
    loc,
    misc_send,
    misc_recv,
    gain_send,
    gain_recv,
    a2a_send,
    a2a_recv,
    *sems,
):
    p = Place()
    g = Gather(
        p,
        (0, 1, 2, 3),
        (wq, wk, wv, wo),
        (wqkv_o, wqkv_o, wqkv_o, wo_o),
        (None, None, None, stage_o),
        sems,
    )
    greet(
        [p.sib()]
        + [p.dev(dy=dy, core=core) for dy in (-1, 1) for core in (0, 1)]
        + context_peers(p)
    )
    gain_targets = [p.sib()] + [p.dev(dy=1, core=core) for core in (0, 1)]
    gain_copies = [
        remote(gain_ref, gains_o.at[p.s], gain_send.at[i], gain_recv.at[i if i == 0 else 1 + p.c], d)
        for i, d in enumerate(gain_targets)
    ]
    for c in gain_copies:
        c.start()
    x_own = pltpu.make_async_copy(x_ref, x_all.at[:, 0], loc.at[0])
    x_own.start()
    x_out = remote(x_ref, x_all.at[:, 1], misc_send.at[0], misc_recv.at[0], p.sib())
    x_out.start()
    g.start()
    gain_own = pltpu.make_async_copy(gain_ref, gains_o.at[p.s], loc.at[1])
    gain_own.start()
    meta_own = pltpu.make_async_copy(meta_ref, meta_o.at[p.c], loc.at[2])
    meta_own.start()
    meta_out = remote(meta_ref, meta_o.at[p.c], misc_send.at[1], misc_recv.at[1], p.sib())
    meta_out.start()
    cot_in = pltpu.make_async_copy(cot_ref, stage_cot, loc.at[3])
    cot_in.start()
    cot_own = pltpu.make_async_copy(stage_cot, cot_o.at[:, 0], loc.at[3])
    cot_out = remote(cot_ref, cot_o.at[:, 1], misc_send.at[2], misc_recv.at[2], p.sib())
    cot_out.start()

    gain_own.wait()
    for i in range(3):
        block = p.yl * 2 + 1 - p.c if i == 0 else (1 - p.yl) * 2 + (i - 1)
        here = gains_o.at[block]
        remote(here, here, gain_send.at[i], gain_recv.at[i], p.sib()).wait_recv()
    x_own.wait()
    x_out.wait_recv()
    gain = jnp.concatenate([gains_o[b, 0:1, :] for b in range(4)], axis=1)

    def norm_step(i, carry):
        v = x_all[i // 2, i % 2].astype(F32).reshape(BLOCK, MODEL)
        r = lax.rsqrt(jnp.mean(v * v, axis=1, keepdims=True) + NORM_EPS)
        v = (v * r * gain).astype(BF)
        attn_in[i // 2, pl.ds((i % 2) * BLOCK, BLOCK), :] = v
        attn_in_t_o[:, pl.ds(pl.multiple_of(i * BLOCK, BLOCK), BLOCK)] = v.T
        return carry

    lax.fori_loop(0, 8, norm_step, 0)
    for i in range(4):
        g.pass_on(i)
    cot_in.wait()
    cot_own.start()

    def send_block(j, q):
        other = p.c if q == 0 else 1 - p.c
        k = j * 2 + other
        slot = j * 2 + q
        return (
            k,
            remote(
                qkv_send.at[slot],
                qkv_o.at[p.k],
                a2a_send.at[slot],
                a2a_recv.at[p.k],
                p.member(k),
            ),
            pltpu.make_async_copy(qkv_send.at[slot], qkv_o.at[p.k], a2a_send.at[slot]),
        )

    for i in range(3):
        g.arrive(i)

    def wide(v):
        v = jnp.concatenate([v, v], axis=1)
        return jnp.concatenate([v, v], axis=0)

    def qkv_step(j, carry):
        a = attn_in[j]
        for part in range(3):
            cols = pl.ds(part * 256, 256)
            w = wqkv_o[:, :, cols].reshape(MODEL, 256)
            v = jnp.dot(a, w, preferred_element_type=F32)
            if part < 2:
                v = v * wide(rope_ref[0]) + swap_halves(v) * wide(rope_ref[1])
            v = v.reshape(32, 8, 256).astype(BF)
            qkv_send[j * 2, :, :, cols] = v[:16]
            qkv_send[j * 2 + 1, :, :, cols] = v[16:]
        for q in (0, 1):
            k, out, here = send_block(j, q)

            @pl.when(k != p.k)
            def _():
                out.start()

            @pl.when(k == p.k)
            def _():
                here.start()

        return carry

    lax.fori_loop(0, 4, qkv_step, 0)
    g.arrive(3)
    for i in range(4):
        g.sent(i)
    x_out.wait_send()
    meta_own.wait()
    meta_out.wait_send()
    here = meta_o.at[1 - p.c]
    remote(here, here, misc_send.at[1], misc_recv.at[1], p.sib()).wait_recv()
    cot_own.wait()
    cot_out.wait()
    for c in gain_copies:
        c.wait_send()
    for j in range(4):
        for q in (0, 1):
            k, out, here = send_block(j, q)

            @pl.when(k != p.k)
            def _():
                out.wait_send()

            @pl.when(k == p.k)
            def _():
                here.wait()

    for i in range(8):

        @pl.when(i != p.k)
        def _():
            here = qkv_o.at[i]
            remote(here, here, a2a_send.at[i], a2a_recv.at[i], p.member(i)).wait_recv()


def start_call(x, cot, weights, gains, meta, rope_own):
    shapes = (
        jax.ShapeDtypeStruct((256, 8, 768), BF),
        jax.ShapeDtypeStruct((32, 8, 2048), BF),
        jax.ShapeDtypeStruct((4, 8, 512), F32),
        jax.ShapeDtypeStruct((2, 8, 1024), jnp.int32),
        jax.ShapeDtypeStruct((4, 2, 16, 8, MODEL), BF),
        jax.ShapeDtypeStruct((MODEL, 1024), BF),
        jax.ShapeDtypeStruct((8, 16, 8, 768), BF),
    )
    return pl.pallas_call(
        start_kernel,
        out_shape=shapes,
        in_specs=[ANY] * 6 + [VM, ANY, VM],
        out_specs=[VM, ANY, VM, ANY, ANY, VM, ANY],
        scratch_shapes=[
            pltpu.VMEM((4, 256, MODEL), BF),
            pltpu.VMEM((4, 2, 16, 8, MODEL), BF),
            pltpu.VMEM((8, 16, 8, 768), BF),
            pltpu.VMEM((32, 8, 512), BF),
            pltpu.VMEM((4, 16, 8, MODEL), BF),
            DMA((4,)),
            DMA((3,)),
            DMA((3,)),
            DMA((3,)),
            DMA((3,)),
            DMA((8,)),
            DMA((8,)),
        ]
        + Gather.sems(4),
        compiler_params=params(1),
    )(tiles(x), tiles(cot), *[tiles(w) for w in weights], gains, meta, rope_own)


def bias_rows(qb, rows, prow, vrow, pcol):
    i = qb * rows + lax.broadcasted_iota(jnp.int32, (rows, 1024), 0)
    j = lax.broadcasted_iota(jnp.int32, (rows, 1024), 1)
    same = (pcol >= 0) & (pcol == prow)
    ok = ((j <= i) | same) & ((vrow > 0) | (i == j))
    return jnp.where(ok, 0.0, MASK_FILL)


def attend_kernel(
    qkv, info, pcol, out_o, lse_o, o_send, a2a_send, a2a_recv
):
    p = Place()
    greet(context_peers(p))
    mine = p.slot(p.k)
    rows = 256

    def sends(i):
        return (
            remote(o_send.at[i], out_o.at[mine], a2a_send.at[i], a2a_recv.at[p.k], p.member(i)),
            pltpu.make_async_copy(o_send.at[i], out_o.at[mine], a2a_send.at[i]),
        )

    def step(qb, carry):
        at = pl.ds(pl.multiple_of(qb * rows, rows), rows)
        bias = bias_rows(qb, rows, info[0:1, :], info[1:2, :], pcol[at, 0:1])
        lane = lax.broadcasted_iota(jnp.int32, (rows, 128), 1)
        totals = jnp.zeros((rows, 128), F32)
        outs = []
        for h in range(4):
            q = qkv[at, pl.ds(h * 64, 64)]
            k = qkv[:, pl.ds(256 + h * 64, 64)]
            v = qkv[:, pl.ds(512 + h * 64, 64)]
            sc = lax.dot_general(q, k, (((1,), (1,)), ((), ())), preferred_element_type=F32)
            sc = sc * (HEAD_DIM**-0.5) + bias
            top = jnp.max(sc, axis=1, keepdims=True)
            e = jnp.exp(sc - top)
            total = jnp.sum(e, axis=1, keepdims=True)
            prob = (e * (1.0 / total)).astype(BF)
            totals = jnp.where(lane == h, top + jnp.log(total), totals)
            outs.append(jnp.dot(prob, v, preferred_element_type=F32))
        lse_o[at, :] = totals
        o = jnp.concatenate(outs, axis=1).reshape(32, 8, 256).astype(BF)
        for half in (0, 1):
            i = qb * 2 + half
            o_send[i] = o[half * 16 : (half + 1) * 16]
            out, here = sends(i)

            @pl.when(i != p.k)
            def _():
                out.start()

            @pl.when(i == p.k)
            def _():
                here.start()

        return carry

    lax.fori_loop(0, 4, step, 0)
    for i in range(8):
        out, here = sends(i)

        @pl.when(i != p.k)
        def _():
            out.wait_send()
            spot = out_o.at[p.slot(i)]
            remote(spot, spot, a2a_send.at[i], a2a_recv.at[i], p.member(i)).wait_recv()

        @pl.when(i == p.k)
        def _():
            here.wait()


def attend_call(qkv, info, pcol):
    return pl.pallas_call(
        attend_kernel,
        out_shape=(
            jax.ShapeDtypeStruct((8, 16, 8, 256), BF),
            jax.ShapeDtypeStruct((1024, 128), F32),
        ),
        in_specs=[VM] * 3,
        out_specs=[ANY, VM],
        scratch_shapes=[pltpu.VMEM((8, 16, 8, 256), BF), DMA((8,)), DMA((8,))],
        compiler_params=params(2),
    )(qkv, info, pcol)


X_SCRATCH = [
    pltpu.VMEM((4, BLOCK, MODEL), F32),
    pltpu.VMEM((4, BLOCK, MODEL), BF),
    pltpu.VMEM((4, BLOCK, MODEL), BF),
    pltpu.VMEM((3, BLOCK, MODEL), BF),
    pltpu.VMEM((3, BLOCK, MODEL), BF),
    DMA((4,)),
    DMA((4,)),
    DMA((6,)),
    DMA((6,)),
    DMA((10,)),
    DMA((10,)),
]


def x_peers(p):
    return [p.sib(), p.dev(dx=1), p.dev(dx=-1)]


def multiplier(lhs, rhs, transposed):
    def multiply(n, j, first):
        cols = pl.ds(pl.multiple_of(first, TILE), TILE)
        if transposed:
            return lax.dot_general(
                lhs[j], rhs[cols, :], (((1,), (1,)), ((), ())), preferred_element_type=F32
            )
        return jnp.dot(lhs[j], rhs[:, cols], preferred_element_type=F32)

    return multiply


def x_phase(p, multiply, scratch, out, both, finish, prepare=None, arrived=None):
    acc, sib_out, sib_in, x_out, x_in, s_send, s_recv, x_send, x_recv, g_send, g_recv = scratch
    half = BLOCK // 2
    top, low = pl.ds(0, half), pl.ds(half, half)
    to_right, to_left = p.dev(dx=1), p.dev(dx=-1)

    def sib_copy(r):
        return remote(sib_out.at[r], sib_in.at[r], s_send.at[r], s_recv.at[r], p.sib())

    def product(r):
        j = (p.x + r) % 4
        n = (2, 1, 3, 0).index(r)
        if prepare is not None:
            prepare(n, j)

        def step(i, carry):
            cols = pl.ds(pl.multiple_of(i * TILE, TILE), TILE)
            v = multiply(n, j, i * TILE)
            acc[r, :, cols] = v[:BLOCK]
            sib_out[r, :, cols] = v[BLOCK:].astype(BF)
            return carry

        lax.fori_loop(0, MODEL // TILE, step, 0)
        sib_copy(r).start()

    def along(n, slot, rows, device):
        return remote(
            x_out.at[slot, rows], x_in.at[slot, rows], x_send.at[n], x_recv.at[n], device
        )

    far_right, far_left = along(0, 0, top, to_right), along(1, 0, low, to_left)
    right_low, right_top = along(2, 1, low, to_right), along(3, 1, top, to_right)
    left_top, left_low = along(4, 2, top, to_left), along(5, 2, low, to_left)
    product(2)
    yield
    product(1)
    sib_copy(2).wait_recv()
    x_out[0] = (acc[2] + sib_in[2].astype(F32)).astype(BF)
    far_right.start()
    far_left.start()
    yield
    product(3)
    sib_copy(1).wait_recv()
    x_out[1, half:] = (acc[1, half:] + sib_in[1, half:].astype(F32)).astype(BF)
    right_low.start()
    sib_copy(3).wait_recv()
    x_out[2, 0:half] = (acc[3, 0:half] + sib_in[3, 0:half].astype(F32)).astype(BF)
    left_top.start()
    yield
    product(0)
    yield
    far_right.wait_recv()
    x_out[1, 0:half] = (
        acc[1, 0:half] + sib_in[1, 0:half].astype(F32) + x_in[0, 0:half].astype(F32)
    ).astype(BF)
    right_top.start()
    far_left.wait_recv()
    x_out[2, half:] = (
        acc[3, half:] + sib_in[3, half:].astype(F32) + x_in[0, half:].astype(F32)
    ).astype(BF)
    left_low.start()
    yield
    sib_copy(0).wait_recv()
    acc[0] += sib_in[0].astype(F32)
    for c in (right_low, left_top, right_top, left_low):
        c.wait_recv()
    total = acc[0] + x_in[1].astype(F32) + x_in[2].astype(F32)
    for r in range(4):
        sib_copy(r).wait_send()
    for c in (far_right, far_left, right_low, right_top, left_top, left_low):
        c.wait_send()

    me, right, left, far = p.x, (p.x + 1) % 4, (p.x + 3) % 4, (p.x + 2) % 4
    out[me, 0] = finish(total)
    sent = []

    def copy(n, j, rows, d):
        src = out.at[j, 0, rows]
        return remote(src, src, g_send.at[n], g_recv.at[n], d)

    def go(c):
        c.start()
        sent.append(c)

    def to_sib(n, j):
        return remote(out.at[j, 0], out.at[j, 1], g_send.at[n], g_recv.at[n], p.sib())

    go(copy(0, me, top, to_right))
    go(copy(1, me, low, to_left))
    go(copy(2, me, low, to_right))
    go(copy(3, me, top, to_left))
    if both:
        go(to_sib(6, me))
    yield
    copy(0, left, top, to_left).wait_recv()
    go(copy(4, left, top, to_right))
    copy(1, right, low, to_right).wait_recv()
    go(copy(5, right, low, to_left))
    yield
    copy(2, left, low, to_left).wait_recv()
    copy(3, right, top, to_right).wait_recv()
    if both:
        go(to_sib(7, left))
        go(to_sib(8, right))
    yield
    copy(4, far, top, to_left).wait_recv()
    copy(5, far, low, to_right).wait_recv()
    if both:
        go(to_sib(9, far))
        yield
        for n, j in ((6, me), (7, left), (8, right), (9, far)):
            to_sib(n, j).wait_recv()
            if arrived is not None:
                arrived(j)
    for c in sent:
        c.wait_send()


def rms(v):
    return lax.rsqrt(jnp.mean(v * v, axis=1, keepdims=True) + NORM_EPS)


def full_row(gains, row):
    return jnp.concatenate([gains[b, row : row + 1, :] for b in range(4)], axis=1)


def norm_back(grad, normed, gain, inv):
    w = grad * gain
    return inv * (w - normed * jnp.mean(w * normed, axis=1, keepdims=True))


UNITS = {
    "down_a": (64, 512, "col", 0, ()),
    "down_b": (64, 512, "col", 64, ()),
    "gate_a": (64, 512, "row", 0, (1024,)),
    "gate_b": (64, 512, "row", 512, (1024,)),
    "up_a": (64, 512, "row", 0, (1024,)),
    "up_b": (64, 512, "row", 512, (1024,)),
    "out": (32, 512, "col", 0, ()),
    "qkv": (64, 768, "row", 0, (256, 256, 256)),
}
UNIT_SCRATCH = 8
DOWN_OUT = jax.ShapeDtypeStruct((2, 2, 2, 32, 8, 512), BF)
OUT_OUT = jax.ShapeDtypeStruct((2, 1, 2, 16, 8, 512), BF)
FFN_OUT = jax.ShapeDtypeStruct((2, 32, 8, 2048), BF)
QKV_OUT = jax.ShapeDtypeStruct((2, 32, 8, 512), BF)


def unit_scratch(name):
    r, c, _, _, _ = UNITS[name]
    return [
        pltpu.VMEM((2, 2, r // 2, 8, c), BF),
        pltpu.VMEM((2, 2, r // 2, 8, c), BF),
        pltpu.VMEM((2, 2, 2, r // 8, 8, c), BF),
        pltpu.VMEM((3, 2, 2, r // 8, 8, c), BF),
        pltpu.VMEM((2, 2, r // 8, 8, c), BF),
        DMA((4,)),
        DMA((18,)),
        DMA((18,)),
    ]


def unit_peers(p):
    return [p.sib(), p.dev(dy=1), p.dev(dy=-1), p.dev(dy=2), p.dev(dz=1), p.dev(dz=-1)]


def unit(p, name, src, outs, scratch):
    rows, cols, kind, first, widths = UNITS[name]
    own, yin, zout, zin, yhin, loc, send, recv = scratch
    part = rows // 8
    half = rows // 2
    z_of = {0: p.dev(dz=1), 1: p.dev(dz=-1)}
    me, zr, zl, zf = p.z, (p.z + 1) % 4, (p.z + 3) % 4, (p.z + 2) % 4

    def cp(n, src, dst, d):
        return remote(src, dst, send.at[n], recv.at[n], d)

    def fetch(yl, h, dst, make):
        if kind == "row":
            return [
                make(
                    h * 2,
                    src.at[pl.ds(yl * 2, 2), pl.ds(h * half, half), :, pl.ds(first, cols)],
                    dst.at[:, h],
                )
            ]
        return [
            make(
                h * 2 + core,
                src.at[pl.ds(first + h * half, half), :, pl.ds((yl * 2 + core) * cols, cols)],
                dst.at[core, h],
            )
            for core in (0, 1)
        ]

    along_y, local = [], []
    for h in (0, 1):
        d = p.dev(dy=1 if h == 0 else -1)
        along_y += fetch(1 - p.yl, h, yin, lambda n, a, b, d=d: cp(n, a, b, d))
        local += fetch(p.yl, h, own, lambda n, a, b: pltpu.make_async_copy(a, b, loc.at[n]))
    for c in along_y + local:
        c.start()
    yield
    for c in local:
        c.wait()
    for c in along_y:
        c.wait_recv()
    own[...] = (own[...].astype(F32) + yin[...].astype(F32)).astype(BF)

    def chunk(h, zc):
        return own.at[:, h, pl.ds(zc * part, part)]

    far = [cp(4 + h, chunk(h, zf), zin.at[0, :, h], z_of[h]) for h in (0, 1)]
    for c in far:
        c.start()
    yield
    for c in far:
        c.wait_send()
    near = []
    for side, zc in ((0, zr), (1, zl)):
        zout[side, :, 1 - side] = own[:, 1 - side, pl.ds(zc * part, part)]
        far[side].wait_recv()
        zout[side, :, side] = (
            own[:, side, pl.ds(zc * part, part)].astype(F32) + zin[0, :, side].astype(F32)
        ).astype(BF)
        c = cp(6 + side, zout.at[side], zin.at[1 + side], z_of[side])
        c.start()
        near.append(c)
    yield
    for c in near:
        c.wait_recv()
    for c in near:
        c.wait_send()
    v = own[:, :, pl.ds(me * part, part)].astype(F32)
    zout[0] = (v + zin[1].astype(F32) + zin[2].astype(F32)).astype(BF)
    yh = cp(8, zout.at[0], yhin, p.dev(dy=2))
    yh.start()
    yield
    yh.wait_recv()
    own[:, :, pl.ds(me * part, part)] = (zout[0].astype(F32) + yhin[...].astype(F32)).astype(BF)
    back = [cp(9 + side * 2 + h, chunk(h, me), chunk(h, me), z_of[side]) for side, h in ((0, 0), (1, 1), (0, 1), (1, 0))]
    for c in back:
        c.start()
    yield
    for side, zc in ((0, zl), (1, zr)):
        here = chunk(side, zc)
        cp(9 + side * 3, here, here, z_of[1 - side]).wait_recv()
        c = cp(13 + side, here, here, z_of[side])
        c.start()
        back.append(c)
    yield
    for side, zc in ((0, zl), (1, zr)):
        here = chunk(1 - side, zc)
        cp(9 + side * 2 + 1 - side, here, here, z_of[1 - side]).wait_recv()
    for h in (0, 1):
        here = chunk(h, zf)
        cp(13 + h, here, here, z_of[1 - h]).wait_recv()
    for c in back + along_y + [yh]:
        c.wait_send()
    done = []
    if kind == "col":
        spot = outs[0].at[p.c, first // rows]
        done.append(cp(15, own.at[1 - p.c], spot, p.sib()))
        done.append(pltpu.make_async_copy(own.at[p.c], spot, loc.at[0]))
    else:
        for i, width in enumerate(widths):
            take = min(cols, width)
            spot = outs[i].at[:, :, :, pl.ds(p.c * width + first, take)]
            piece = pl.ds(i * take, take)
            done.append(cp(15 + i, own.at[1 - p.c, :, :, :, piece], spot, p.sib()))
            done.append(pltpu.make_async_copy(own.at[p.c, :, :, :, piece], spot, loc.at[i]))
    for c in done:
        c.start()
    yield
    for c in done:
        c.wait()


def out_proj_kernel(
    lhs,
    rhs,
    x_own,
    keep,
    gains,
    wg,
    wu,
    wd,
    ffn_in_o,
    resid_o,
    stat_o,
    wgu_o,
    wd_o,
    stage_g,
    stage_u,
    stage_d,
    *scratch,
):
    p = Place()
    nx = len(X_SCRATCH)
    g = Gather(
        p,
        (4, 5, 6),
        (wg, wu, wd),
        (wgu_o, wgu_o, wd_o),
        (stage_g, stage_u, stage_d),
        scratch[nx:],
    )
    greet(Gather.peers(p) + [p.dev(dx=1), p.dev(dx=-1)])

    def finish(attn_out):
        stat_o[...] = jnp.full((8, 128), jnp.sum(keep[:, 0:1] * attn_out * attn_out), F32)
        resid = x_own[...].astype(F32) + attn_out
        resid_o[...] = resid
        return (resid * rms(resid) * full_row(gains, 1)).astype(BF)

    run(
        PROJ_ORDER,
        g=g.steps(),
        x=x_phase(p, multiplier(lhs, rhs, False), scratch[:nx], ffn_in_o, True, finish),
    )


def out_proj_call(lhs, rhs, x_own, keep, gains, weights):
    return pl.pallas_call(
        out_proj_kernel,
        out_shape=(
            jax.ShapeDtypeStruct((4, 2, BLOCK, MODEL), BF),
            jax.ShapeDtypeStruct((BLOCK, MODEL), F32),
            jax.ShapeDtypeStruct((8, 128), F32),
            jax.ShapeDtypeStruct((256, 8, 2048), BF),
            jax.ShapeDtypeStruct((128, 8, 2048), BF),
        ),
        in_specs=[VM] * 5 + [ANY] * 3,
        out_specs=[VM] * 3 + [ANY] * 2,
        scratch_shapes=[
            pltpu.VMEM((64, 8, 1024), BF),
            pltpu.VMEM((64, 8, 1024), BF),
            pltpu.VMEM((128, 8, 512), BF),
        ]
        + X_SCRATCH
        + Gather.sems(3),
        compiler_params=params(3),
    )(lhs, rhs, x_own, keep, gains, *[tiles(w) for w in weights])


def ffn_kernel(a_ref, c_ref, wg, wu, wd, h_o, gg_o, gu_o, dd_o, dg_o, du_o, a_t):
    rows = FFN_ROWS

    @pl.when(pl.program_id(0) == 0)
    def _():
        def turn(i, carry):
            at = pl.ds(pl.multiple_of(i * 256, 256), 256)
            a_t[:, at] = a_ref[at, :].T
            return carry

        lax.fori_loop(0, 4, turn, 0)

    def step(i, carry):
        at = pl.ds(pl.multiple_of(i * rows, rows), rows)
        a = a_ref[at, :]
        gate = jnp.dot(a, wg[...], preferred_element_type=F32)
        up = jnp.dot(a, wu[...], preferred_element_type=F32)
        grad = lax.dot_general(
            c_ref[at, :], wd[...], (((1,), (1,)), ((), ())), preferred_element_type=F32
        )
        sig = 1.0 / (1.0 + jnp.exp(-gate))
        silu = gate * sig
        h_o[at, :] = (silu * up).astype(BF)
        gg_o[at, :] = (grad * up * sig * (1.0 + gate * (1.0 - sig))).astype(BF)
        gu_o[at, :] = (grad * silu).astype(BF)
        return carry

    lax.fori_loop(0, 1024 // rows, step, 0)
    h_t = h_o[...].T

    def down(n, carry):
        cols = pl.ds(pl.multiple_of(n * 256, 256), 256)
        dd_o[:, cols] = jnp.dot(h_t, c_ref[:, cols], preferred_element_type=F32).astype(BF)
        return carry

    lax.fori_loop(0, MODEL // 256, down, 0)

    def back(n, carry):
        at = pl.ds(pl.multiple_of(n * FFN_BACK, FFN_BACK), FFN_BACK)
        t = a_t[at, :]
        dg_o[at, :] = jnp.dot(t, gg_o[...], preferred_element_type=F32).astype(BF)
        du_o[at, :] = jnp.dot(t, gu_o[...], preferred_element_type=F32).astype(BF)
        return carry

    lax.fori_loop(0, MODEL // FFN_BACK, back, 0)


def ffn_call(ffn_in, cot, wgu, wd):
    tile = FFN_TILE
    n = 1024 // tile
    whole = pl.BlockSpec((1024, MODEL), lambda i: (0, 0), pipeline_mode=pl.Buffered(1))
    cols = pl.BlockSpec((1024, tile), lambda i: (0, i))
    tall = pl.BlockSpec((MODEL, tile), lambda i: (0, i))
    wide = pl.BlockSpec((tile, MODEL), lambda i: (i, 0))
    tokens = jax.ShapeDtypeStruct((1024, 1024), BF)
    grads = jax.ShapeDtypeStruct((MODEL, 1024), BF)
    return pl.pallas_call(
        ffn_kernel,
        grid=(n,),
        out_shape=(tokens, tokens, tokens, jax.ShapeDtypeStruct((1024, MODEL), BF), grads, grads),
        in_specs=[whole, whole, tall, pl.BlockSpec((MODEL, tile), lambda i: (0, i + n)), wide],
        out_specs=[cols, cols, cols, wide, tall, tall],
        scratch_shapes=[pltpu.VMEM((MODEL, 1024), BF)],
        compiler_params=params(),
    )(ffn_in, cot, wgu, wgu, wd)


MID = ("down_a", "down_b", "gate_a", "gate_b")


def mid_kernel(*refs):
    gate, up, hidden, wgu, wd, dd, dgate = refs[:7]
    wo, resid_ref, cot_own, gains, keep, qkv, info, pcol, lse, rope = refs[7:17]
    grad_o, resid_grad_o, gain_o, final_o, stat_o, d_o, dd_o, dgate_o = refs[17:25]
    lhs, rhs, g_out, g_in, d_out, dk, dv = refs[25:32]
    loc, g_send, g_recv, a2a_send, a2a_recv = refs[32:37]
    at = 37
    nx = len(X_SCRATCH)
    xs = refs[at : at + nx]
    at += nx
    us = [refs[at + i * UNIT_SCRATCH : at + (i + 1) * UNIT_SCRATCH] for i in range(len(MID))]
    p = Place()
    greet(context_peers(p) + x_peers(p) + [p.dev(dy=1), p.dev(dy=-1)])
    rows = ATTEND_ROWS
    each = rows // 8
    scale = HEAD_DIM**-0.5
    mine = p.slot(p.k)

    def fetch(n, sources):
        j = (p.x + (2, 1, 3, 0)[n]) % 4
        return [
            pltpu.make_async_copy(v.at[j], lhs.at[n % 2, i], loc.at[(n % 2) * 2 + i])
            for i, v in enumerate(sources)
        ]

    def preparer(sources, right):
        def prepare(n, j):
            if n == 0:
                for c in fetch(0, sources):
                    c.start()
            if n < 3:
                for c in fetch(n + 1, sources):
                    c.start()
            if n == 0:
                right.wait()
            for c in fetch(n, sources):
                c.wait()

        return prepare

    def flat(v):
        return v.reshape(v.shape[0] * 8, v.shape[2])

    wgu_in = pltpu.make_async_copy(wgu, rhs, loc.at[4])
    wgu_in.start()
    wd_in = pltpu.make_async_copy(wd, rhs.at[pl.ds(0, 128)], loc.at[4])

    def multiply_back(n, j, first):
        v = 0.0
        for i in (0, 1):
            w = rhs[pl.ds(first // 8, TILE // 8), :, pl.ds(i * 1024, 1024)]
            v += lax.dot_general(
                flat(lhs[n % 2, i]), flat(w), (((1,), (1,)), ((), ())), preferred_element_type=F32
            )
        return v

    def multiply_out(n, j, first):
        w = rhs[pl.ds(0, 128), :, pl.ds(pl.multiple_of(first, TILE), TILE)]
        return jnp.dot(flat(lhs[n % 2, 0]), flat(w), preferred_element_type=F32)

    def finish_back(g):
        wd_in.start()
        resid = resid_ref[...]
        inv = rms(resid)
        normed = resid * inv
        gain_o[...] = jnp.broadcast_to(jnp.sum(g * normed, axis=0, keepdims=True), (8, MODEL))
        grad_resid = cot_own[...].astype(F32) + norm_back(g, normed, full_row(gains, 1), inv)
        resid_grad_o[...] = grad_resid
        return grad_resid.astype(BF)

    def finish_out(ffn_out):
        final = resid_ref[...] + ffn_out
        kp = keep[:, 0:1]
        stat_o[0] = jnp.full((8, 128), jnp.sum(kp * ffn_out * ffn_out), F32)
        stat_o[1] = jnp.full((8, 128), jnp.sum(kp * final * final), F32)
        return final.astype(BF)

    def g_copy(j, q):
        k = j * 2 + (p.c if q == 0 else 1 - p.c)
        slot = j * 2 + q
        return (
            k,
            remote(g_out.at[slot], g_in.at[p.k], g_send.at[slot], g_recv.at[p.k], p.member(k)),
            pltpu.make_async_copy(g_out.at[slot], g_in.at[p.k], g_send.at[slot]),
        )

    def arrived(j):
        v = lax.dot_general(
            grad_o[j].reshape(256, MODEL), wo[...], (((1,), (1,)), ((), ())), preferred_element_type=F32
        )
        v = v.reshape(32, 8, 256).astype(BF)
        for q in (0, 1):
            g_out[j * 2 + q] = v[q * 16 : (q + 1) * 16]
            k, out, here = g_copy(j, q)

            @pl.when(k != p.k)
            def _():
                out.start()

            @pl.when(k == p.k)
            def _():
                here.start()

    def sends(i):
        return (
            remote(d_out.at[i], d_o.at[mine], a2a_send.at[i], a2a_recv.at[p.k], p.member(i)),
            pltpu.make_async_copy(d_out.at[i], d_o.at[mine], a2a_send.at[i]),
        )

    def wide(v):
        return jnp.concatenate([v, v], axis=1)

    def query_block(qb):
        spot = pl.ds(qb * rows, rows)
        bias = bias_rows(qb, rows, info[0:1, :], info[1:2, :], pcol[spot, 0:1])
        blocks = pl.ds(qb * (rows // BLOCK), rows // BLOCK)
        g2 = g_in[blocks].astype(F32).reshape(rows, 256).astype(BF)
        dqs = []
        for h in range(4):
            lanes = pl.ds(h * 64, 64)
            q = qkv[spot, lanes]
            k = qkv[:, pl.ds(256 + h * 64, 64)]
            v = qkv[:, pl.ds(512 + h * 64, 64)]
            g = g2[:, h * 64 : (h + 1) * 64]
            sc = lax.dot_general(q, k, (((1,), (1,)), ((), ())), preferred_element_type=F32)
            prob = jnp.exp(sc * scale + bias - lse[spot, h : h + 1])
            gp = lax.dot_general(g, v, (((1,), (1,)), ((), ())), preferred_element_type=F32)
            inner = jnp.sum(prob * gp, axis=1, keepdims=True)
            gs = (prob * (gp - inner)).astype(BF)
            dqs.append(jnp.dot(gs, k, preferred_element_type=F32))
            dk[:, lanes] += lax.dot_general(
                gs, q, (((0,), (0,)), ((), ())), preferred_element_type=F32
            )
            dv[:, lanes] += lax.dot_general(
                prob.astype(BF), g, (((0,), (0,)), ((), ())), preferred_element_type=F32
            )
        dq = jnp.concatenate(dqs, axis=1) * scale
        dq = dq * wide(rope[0, spot]) - swap_halves(dq) * wide(rope[1, spot])
        dq = dq.reshape(each, 8, 256).astype(BF)
        for b in range(rows // BLOCK):
            d_out[qb * (rows // BLOCK) + b, :, :, 0:256] = dq[b * 16 : (b + 1) * 16]

    def give(i, carry):
        spot = pl.ds(pl.multiple_of(i * BLOCK, BLOCK), BLOCK)
        w = dk[spot, :] * scale
        w = w * wide(rope[0, spot]) - swap_halves(w) * wide(rope[1, spot])
        d_out[i, :, :, 256:512] = w.reshape(16, 8, 256).astype(BF)
        d_out[i, :, :, 512:768] = dv[spot, :].reshape(16, 8, 256).astype(BF)
        out, here = sends(i)

        @pl.when(i != p.k)
        def _():
            out.start()

        @pl.when(i == p.k)
        def _():
            here.start()

        return carry

    def main():
        yield from x_phase(
            p,
            multiply_back,
            xs,
            grad_o,
            True,
            finish_back,
            preparer((gate, up), wgu_in),
            arrived,
        )
        dk[...] = jnp.zeros_like(dk)
        dv[...] = jnp.zeros_like(dv)
        yield
        for j in range(4):
            for q in (0, 1):
                k, out, here = g_copy(j, q)

                @pl.when(k != p.k)
                def _():
                    out.wait_send()

                @pl.when(k == p.k)
                def _():
                    here.wait()

        for i in range(8):

            @pl.when(i != p.k)
            def _():
                spot = g_in.at[i]
                remote(spot, spot, g_send.at[i], g_recv.at[i], p.member(i)).wait_recv()

        for qb in range(1024 // rows):
            query_block(qb)
            yield
        lax.fori_loop(0, 8, give, 0)
        yield
        for i in range(8):
            out, here = sends(i)

            @pl.when(i != p.k)
            def _():
                out.wait_send()
                spot = d_o.at[p.slot(i)]
                remote(spot, spot, a2a_send.at[i], a2a_recv.at[i], p.member(i)).wait_recv()

            @pl.when(i == p.k)
            def _():
                here.wait()

    x = x_phase(
        p, multiply_out, xs, final_o, False, finish_out, preparer((hidden,), wd_in)
    )
    a, b, c, d = [
        unit(p, name, src, (o,), scr)
        for name, src, o, scr in zip(MID, (dd, dd, dgate, dgate), (dd_o, dd_o, dgate_o, dgate_o), us)
    ]
    run(MID_ORDER, m=main(), x=x, a=a, b=b, c=c, d=d)


def mid_call(gate, up, hidden, wgu, wd, dd, dgate, wo, *rest):
    scratch = list(X_SCRATCH)
    for name in MID:
        scratch += unit_scratch(name)
    blocks = [tiles(v.reshape(4, 256, 1024)) for v in (gate, up, hidden)]
    return pl.pallas_call(
        mid_kernel,
        out_shape=(
            jax.ShapeDtypeStruct((4, 2, BLOCK, MODEL), BF),
            jax.ShapeDtypeStruct((BLOCK, MODEL), F32),
            jax.ShapeDtypeStruct((8, MODEL), F32),
            jax.ShapeDtypeStruct((4, 1, BLOCK, MODEL), BF),
            jax.ShapeDtypeStruct((2, 8, 128), F32),
            jax.ShapeDtypeStruct((8, 16, 8, 768), BF),
            DOWN_OUT,
            FFN_OUT,
        ),
        in_specs=[ANY] * 7 + [VM] * 10,
        out_specs=[VM] * 5 + [ANY] * 3,
        scratch_shapes=[
            pltpu.VMEM((2, 2, 32, 8, 1024), BF),
            pltpu.VMEM((256, 8, 2048), BF),
            pltpu.VMEM((8, 16, 8, 256), BF),
            pltpu.VMEM((8, 16, 8, 256), BF),
            pltpu.VMEM((8, 16, 8, 768), BF),
            pltpu.VMEM((1024, 256), F32),
            pltpu.VMEM((1024, 256), F32),
            DMA((5,)),
            DMA((8,)),
            DMA((8,)),
            DMA((8,)),
            DMA((8,)),
        ]
        + scratch,
        compiler_params=params(5),
    )(*blocks, wgu, wd, tiles(dd), tiles(dgate).reshape(4, 64, 8, 1024), wo, *rest)


LAST = ("up_a", "up_b", "out", "qkv")


def last_kernel(
    lhs,
    rhs,
    x_own,
    grad_resid,
    gains,
    ffn_gain,
    stat_attn,
    stat_ffn,
    keep,
    attn_in_t,
    attended,
    grad_attn,
    dup,
    *refs,
):
    out_o, small_o, up_o, do_o = refs[:4]
    qkv_o = refs[4:7]
    at = 7
    nx = len(X_SCRATCH)
    xs = refs[at : at + nx]
    at += nx
    us = []
    for _ in LAST:
        us.append(refs[at : at + UNIT_SCRATCH])
        at += UNIT_SCRATCH
    core_in, ring_in, s_send, s_recv, do, dw = refs[at:]
    p = Place()
    greet(unit_peers(p) + [p.dev(dx=1), p.dev(dx=-1), p.dev(dx=2), p.dev(dz=2)])

    def finish(g):
        v = x_own[...].astype(F32)
        inv = rms(v)
        normed = v * inv
        few = slice(0, 128)
        small_o[...] = jnp.zeros_like(small_o)
        small_o[0:1, :] = jnp.sum(g * normed, axis=0, keepdims=True)
        small_o[1:2, :] = ffn_gain[0:1, :]
        small_o[2:3, few] = jnp.sum(keep[...], axis=0, keepdims=True)
        small_o[3:4, few] = stat_attn[0:1, :]
        small_o[4:5, few] = stat_ffn[0, 0:1, :]
        small_o[5:6, few] = stat_ffn[1, 0:1, :]
        grad_in = grad_resid[...] + norm_back(g, normed, full_row(gains, 0), inv)
        return grad_in.astype(BF)

    def small():
        core_in[p.c] = small_o[...]
        c = remote(core_in.at[p.c], core_in.at[p.c], s_send.at[0], s_recv.at[0], p.sib())
        c.start()
        yield
        here = core_in.at[1 - p.c]
        remote(here, here, s_send.at[0], s_recv.at[0], p.sib()).wait_recv()
        c.wait_send()
        total = core_in[0] + core_in[1]
        for axis, me, move in (
            (0, p.x, lambda d: p.dev(dx=d)),
            (1, p.y, lambda d: p.dev(dy=d)),
            (2, p.z, lambda d: p.dev(dz=d)),
        ):
            ring_in[axis, me] = total
            here = ring_in.at[axis, me]
            out = [
                remote(
                    here, here, s_send.at[axis * 3 + d], s_recv.at[axis * 3 + d], move(d)
                )
                for d in (1, 2, 3)
            ]
            for c in out:
                c.start()
            yield
            for d in (1, 2, 3):
                there = ring_in.at[axis, (me + 4 - d) % 4]
                remote(
                    there, there, s_send.at[axis * 3 + d], s_recv.at[axis * 3 + d], move(4 - d)
                ).wait_recv()
            for c in out:
                c.wait_send()
            total = (ring_in[axis, 0] + ring_in[axis, 1]) + (ring_in[axis, 2] + ring_in[axis, 3])
        small_o[...] = total

    def out_unit():
        left = attended[...].reshape(1024, 256).T

        def step(n, carry):
            cols = pl.ds(pl.multiple_of(n * 512, 512), 512)
            v = jnp.dot(left, grad_attn[:, cols], preferred_element_type=F32)
            do[:, :, cols] = v.reshape(32, 8, 512).astype(BF)
            return carry

        lax.fori_loop(0, 4, step, 0)
        yield from unit(p, LAST[2], do, (do_o,), us[2])

    def qkv_unit():
        def step(n, carry):
            v = jnp.dot(
                attn_in_t[pl.ds(pl.multiple_of(n * 512, 512), 512), :],
                lhs[...].reshape(1024, 768),
                preferred_element_type=F32,
            )
            dw[n] = v.reshape(64, 8, 768).astype(BF)
            return carry

        lax.fori_loop(0, 4, step, 0)
        yield from unit(p, LAST[3], dw, qkv_o, us[3])

    run(
        LAST_ORDER,
        x=x_phase(p, multiplier(lhs, rhs, True), xs, out_o, False, finish),
        a=unit(p, LAST[0], dup, (up_o,), us[0]),
        b=unit(p, LAST[1], dup, (up_o,), us[1]),
        c=out_unit(),
        d=qkv_unit(),
        s=small(),
    )


def last_call(lhs, rhs, x_own, grad_resid, gains, small_parts, attn_in_t, attended, grad_attn, dup):
    scratch = list(X_SCRATCH)
    for name in LAST:
        scratch += unit_scratch(name)
    outs = [FFN_OUT, OUT_OUT, QKV_OUT, QKV_OUT, QKV_OUT]
    return pl.pallas_call(
        last_kernel,
        out_shape=(
            jax.ShapeDtypeStruct((4, 1, BLOCK, MODEL), BF),
            jax.ShapeDtypeStruct((8, MODEL), F32),
            *outs,
        ),
        in_specs=[VM] * 12 + [ANY],
        out_specs=[VM] * 2 + [ANY] * len(outs),
        scratch_shapes=scratch
        + [
            pltpu.VMEM((2, 8, MODEL), F32),
            pltpu.VMEM((3, 4, 8, MODEL), F32),
            DMA((10,)),
            DMA((10,)),
            pltpu.VMEM((32, 8, MODEL), BF),
            pltpu.VMEM((4, 64, 8, 768), BF),
        ],
        compiler_params=params(6),
    )(
        lhs,
        rhs,
        x_own,
        grad_resid,
        gains,
        *small_parts,
        attn_in_t,
        attended,
        grad_attn,
        tiles(dup).reshape(4, 64, 8, 1024),
    )


def rope_table():
    half_dim = HEAD_DIM // 2
    inv_freq = ROPE_BASE ** (-np.arange(half_dim) * 2.0 / HEAD_DIM)
    angles = np.arange(1024)[:, None] * inv_freq[None, :]
    cosine, sine = np.cos(angles), np.sin(angles)
    cosine = np.concatenate([cosine, cosine], axis=1)
    sine = np.concatenate([-sine, sine], axis=1)
    return np.stack([np.tile(cosine, (1, 2)), np.tile(sine, (1, 2))]).astype(np.float32)


def piece_index(starts, piece_tags, positions):
    inside = (positions[None, :, None] >= starts[:, None, :]) & (
        positions[None, :, None] < starts[:, None, :] + PIECE
    )
    tagged = jnp.where(inside, piece_tags[:, None, :] + 1, 0)
    return jnp.sum(tagged, axis=2) - 1


def per_device(
    inputs,
    cotangent,
    q_weight,
    k_weight,
    v_weight,
    o_weight,
    gate_weight,
    up_weight,
    down_weight,
    attn_gain,
    ffn_gain,
    piece_starts,
    piece_ids,
    valid_mask,
):
    x_at = lax.axis_index("tensor")
    ctx = lax.axis_index("context")
    positions = jnp.arange(1024, dtype=jnp.int32)
    rope = jnp.asarray(rope_table())
    rope_own = lax.dynamic_slice_in_dim(rope, ctx * BLOCK, BLOCK, 1)
    meta = jnp.concatenate([piece_index(piece_starts, piece_ids, positions), valid_mask], axis=0)
    gains_own = jnp.concatenate(
        [
            attn_gain.astype(F32)[None],
            ffn_gain.astype(F32)[None],
            jnp.zeros((6, attn_gain.shape[0]), F32),
        ],
        axis=0,
    )
    wqkv, wo, gains, meta_all, cot_all, attn_in_t, qkv = start_call(
        inputs,
        cotangent,
        (q_weight, k_weight, v_weight, o_weight),
        gains_own,
        meta,
        rope_own,
    )
    seq = lax.dynamic_slice(meta_all, (ctx % 2, 0, 0), (1, 8, 1024))[0]
    piece_row = lax.dynamic_slice_in_dim(seq, ctx // 2, 1, 0)
    valid_row = lax.dynamic_slice_in_dim(seq, 4 + ctx // 2, 1, 0)
    info = jnp.concatenate([piece_row, valid_row, jnp.zeros((6, 1024), jnp.int32)], axis=0)
    pcol = jnp.broadcast_to(piece_row.reshape(1024, 1), (1024, 128))
    wqkv, wo = rows_of(wqkv), rows_of(wo)
    cot_all = rows_of(cot_all)
    qkv = qkv.reshape(1024, 768)
    attended, lse = attend_call(qkv, info, pcol)
    x_own = lax.dynamic_index_in_dim(inputs, x_at, 0, keepdims=False)
    cot_own = lax.dynamic_index_in_dim(cotangent, x_at, 0, keepdims=False)
    keep_own = lax.dynamic_slice(valid_mask, (x_at, ctx * BLOCK), (1, BLOCK)).astype(F32)
    keep = jnp.broadcast_to(keep_own.reshape(BLOCK, 1), (BLOCK, 128))
    attended = attended.reshape(4, 256, 256)
    ffn_in, resid, stat_attn, wgu, wd = out_proj_call(
        attended, wo, x_own, keep, gains, (gate_weight, up_weight, down_weight)
    )
    ffn_in = ffn_in.reshape(1024, MODEL)
    cot_rows = cot_all.reshape(1024, MODEL)
    hidden, grad_gate, grad_up, dd, dgate, dup = ffn_call(
        ffn_in, cot_rows, rows_of(wgu), rows_of(wd)
    )

    grad_attn, grad_resid, ffn_gain_part, output, stat_ffn, d_seq, sd, sgate = mid_call(
        grad_gate,
        grad_up,
        hidden,
        wgu,
        wd,
        dd,
        dgate,
        wo,
        resid,
        cot_own,
        gains,
        keep,
        qkv,
        info,
        pcol,
        lse,
        rope,
    )
    dqkv = d_seq.reshape(4, 256, 768)
    input_grad, small, sup, so, sq, sk, sv = last_call(
        dqkv,
        wqkv,
        x_own,
        grad_resid,
        gains,
        (ffn_gain_part, stat_attn, stat_ffn, keep),
        attn_in_t,
        attended,
        grad_attn.reshape(1024, MODEL),
        dup,
    )
    grads = [v.reshape(-1, v.shape[-1]).astype(F32) for v in (sq, sk, sv, so, sgate, sup, sd)]
    branch_rms = jnp.sqrt(small[3:6, 0] / (jnp.maximum(small[2, 0], 1.0) * MODEL))
    gain_start = (lax.axis_index("shard") * 4 + x_at) * BLOCK
    attn_gain_out = lax.dynamic_slice(small, (0, gain_start), (1, BLOCK))[0]
    ffn_gain_out = lax.dynamic_slice(small, (1, gain_start), (1, BLOCK))[0]
    return (
        output.reshape(4, BLOCK, MODEL),
        input_grad.reshape(4, BLOCK, MODEL),
        *grads,
        attn_gain_out,
        ffn_gain_out,
        branch_rms,
    )


def solution(mesh):
    return jax.shard_map(
        per_device,
        mesh=mesh,
        in_specs=(
            P("shard", "context", None),
            P("shard", "context", None),
            P("shard", "tensor"),
            P("shard", "tensor"),
            P("shard", "tensor"),
            P("tensor", "shard"),
            P("shard", "tensor"),
            P("shard", "tensor"),
            P("tensor", "shard"),
            P("shard"),
            P("shard"),
            P("shard", None),
            P("shard", None),
            P("shard", None),
        ),
        out_specs=(
            P("shard", "context", None),
            P("shard", "context", None),
            P("shard", "tensor"),
            P("shard", "tensor"),
            P("shard", "tensor"),
            P("tensor", "shard"),
            P("shard", "tensor"),
            P("shard", "tensor"),
            P("tensor", "shard"),
            P(("shard", "tensor")),
            P(("shard", "tensor")),
            P(),
        ),
        check_vma=False,
    )
```

profile of v0, /device:TPU:1, one launch (start us, length us, event | category | flops | bytes accessed | tf_op | source)
XLA Modules:
  0.0 495.0 jit_solution(12795053734100168976)
XLA Ops:
  5.1 1.3 pad_add_fusion.meta_ref
  7.2 1.6 constant_dynamic-slice_fusion.2.rope_ref
  8.8 2.3 dynamic-slice_bitcast_fusion
  11.0 54.8 %shard_map.238 = (bf16[256,8,768]{2,1,0:T(8,128)(2,1)}, bf16[32,8,2048]{2,1,0:T(8,128)(2,1)}, f32[4,8,512]{2,1,0:T(8,128)}, s32[2,8,1024]{2,1,0:T(8,128)}, bf16[...) custom-call(bf16[4,16,8,2048]{3,2,1,0:T(8,128)(2,1)} %bitcast.78, ...), custom_call_target="tpu_custom_call" | custom-call | tf_op jit(solution)/shard_map/pallas_call | solution.py:459
  65.8 0.9 constant_dynamic-slice_fusion.1
  67.3 1.0 broadcast_in_dim.58.pcol.refs_14_
  68.3 25.0 %shard_map.239 = (bf16[8,16,8,256]{3,2,1,0:T(8,128)(2,1)}, f32[1024,128]{1,0:T(8,128)}) custom-call(bf16[1024,768]{1,0:T(8,128)(2,1)} %bitcast.68, s32[8,1024]{1,0:T(8,128)} %add_add_fusion.info.refs_13_, s32[1024,128]{1,0:T(8,128)} %broadcast_in_dim.58.pcol.refs_14_), custom_call_target="tpu_custom_call" | custom-call | tf_op jit(solution)/shard_map/pallas_call | solution.py:556
  93.4 64.3 %shard_map.240 = (bf16[4,2,128,2048]{3,2,1,0:T(8,128)(2,1)}, f32[128,2048]{1,0:T(8,128)}, f32[8,128]{1,0:T(8,128)}, bf16[256,8,2048]{2,1,0:T(8,128)(2,1)}, bf16[128,8,2048]{2,1,0:T(8,128)(2,1)}) custom-call(bf16[4,256,256]{2,1,0:T(8,128)(2,1)} %bitcast.84, bf16[256,2048]{1,0:T(8,128)(2,1)} %bitcast.76, bf16[128,2048]{1,0:T(8,128)(2,1)} %get-tuple-element.89.x_own, ...), custom_call_target="tpu_custom_call" | custom-call | tf_op jit(solution)/shard_map/pallas_call | solution.py:923
  157.7 41.1 %shard_map.241 = (bf16[1024,1024]{1,0:T(8,128)(2,1)}, bf16[1024,1024]{1,0:T(8,128)(2,1)}, bf16[1024,1024]{1,0:T(8,128)(2,1)}, bf16[1024,2048]{1,0:T(8,128)(2,1)}...) custom-call(bf16[1024,2048]{1,0:T(8,128)(2,1)} %bitcast.75, bf16[1024,2048]{1,0:T(8,128)(2,1)} %bitcast.71, ...), custom_call_target="tpu_custom_call" | custom-call | tf_op jit(solution)/shard_map/pallas_call | solution.py:1001
  198.9 134.5 %shard_map.242 = (bf16[4,2,128,2048]{3,2,1,0:T(8,128)(2,1)}, f32[128,2048]{1,0:T(8,128)}, f32[8,2048]{1,0:T(8,128)}, bf16[4,1,128,2048]{3,2,1,0:T(8,128)(2,1)}, ...) custom-call(bf16[4,32,8,1024]{3,2,1,0:T(8,128)(2,1)} %bitcast.82, ...), custom_call_target="tpu_custom_call" | custom-call | tf_op jit(solution)/shard_map/pallas_call | solution.py:1241
  333.4 138.1 %shard_map.243 = (bf16[4,1,128,2048]{3,2,1,0:T(8,128)(2,1)}, f32[8,2048]{1,0:T(8,128)}, bf16[2,32,8,2048]{3,2,1,0:T(8,128)(2,1)}, bf16[2,1,2,16,8,512]{5,4,3,2,1...) custom-call(bf16[4,256,768]{2,1,0:T(8,128)(2,1)} %bitcast.91, ...), custom_call_target="tpu_custom_call" | custom-call | tf_op jit(solution)/shard_map/pallas_call | solution.py:1398
  471.5 1.2 slice.7
  473.4 1.3 sqrt_reduce_fusion
  474.7 1.3 dynamic-slice_bitcast_fusion.3
  476.1 2.2 bitcast_convert_fusion.6
  478.3 2.3 bitcast_convert_fusion.5
  480.6 1.1 bitcast_convert_fusion.4
  481.7 1.1 bitcast_convert_fusion.3
  482.9 2.7 bitcast_convert_fusion.1
  485.5 2.7 bitcast_convert_fusion.2
  488.2 2.7 bitcast_convert_fusion
  491.0 1.3 copy.35
  492.3 1.0 copy-done.4
  493.3 1.3 copy.36
  (26 shorter events, 5.8 us)
Async XLA Ops:
  471.5 9.1 %copy-start.6 = (bf16[2,32,8,512]{3,2,1,0:T(8,128)(2,1)S(1)}, bf16[2,32,8,512]{3,2,1,0:T(8,128)(2,1)}, u32[]{:S(2)}) copy-start(bf16[2,32,8,512]{3,2,1,0:T(8,128)(2,1)} %get-tuple-element.76) | copy-start | bytes 1572868
  476.1 5.6 %copy-start.5 = (bf16[2,1,2,16,8,512]{5,4,3,2,1,0:T(8,128)(2,1)S(1)}, bf16[2,1,2,16,8,512]{5,4,3,2,1,0:T(8,128)(2,1)}, u32[]{:S(2)}) copy-start(bf16[2,1,2,16,8,512]{5,4,3,2,1,0:T(8,128)(2,1)} %get-tuple-element.77) | copy-start | bytes 1572868
  478.3 4.6 copy-start.2
  482.9 2.7 copy-start.1
  485.5 2.7 copy-start
  488.2 2.7 copy-start.3
  491.0 2.3 copy-start.4
where the time goes:
time: 502 us; the launch traced here: 495 us
  Pallas kernels  458 us (91%)
  other arithmetic  22.5 us (4%)
  local copies, waits for them, and re-layouts  12.8 us (3%)
    pallas_call x1, Pallas kernels, last_call(): pl.pallas_call(last_kernel, out_shape=(jax.ShapeDtypeStruct((4, 1, BLOCK,...  138 us
    pallas_call x1, Pallas kernels, mid_call(): pl.pallas_call(mid_kernel, out_shape=(jax.ShapeDtypeStruct((4, 2, BLOCK,...  135 us
    pallas_call x1, Pallas kernels, out_proj_call(): pl.pallas_call(out_proj_kernel, out_shape=(jax.ShapeDtypeStruct((4, 2, BL...  64.3 us
    pallas_call x1, Pallas kernels, start_call(): pl.pallas_call(start_kernel, out_shape=shapes, in_specs=[ANY] * 6 + [VM,...  54.8 us
    pallas_call x1, Pallas kernels, ffn_call(): pl.pallas_call(ffn_kernel, grid=(n,), out_shape=(tokens, tokens, tokens,...  41.1 us
    pallas_call x1, Pallas kernels, attend_call(): pl.pallas_call(attend_kernel, out_shape=(jax.ShapeDtypeStruct((8, 16, 8,...  25 us
    convert_element_type x7, other arithmetic, per_device(): v.reshape(-1, v.shape[-1]).astype(F32)  14.9 us

commit v1 on v0

--- a/solution.py
+++ b/solution.py
@@ -19,10 +19,13 @@
 VM = pl.BlockSpec(memory_space=pltpu.VMEM)
 DMA = pltpu.SemaphoreType.DMA
 PROJ_ORDER = "gxxxxxggxgxgxgxggx"
-MID_ORDER = "amcmmammbacmcdbambmdcmbmdxacxxbdmxamdxbmdxcmmxcdbaxdbcaxmbammmxx"
+MID_ORDER = (
+    "amemmcbmmaemadcemmbacmebmxcxdbaxdmeaxxdcmbe"
+    "mcxdbmdmxcabdxecxabdmexdxmbcamme"
+)
 ATTEND_ROWS = 256
-LAST_ORDER = "bxaxdbxxbxabaxcdxbcdxacsbadsbxsaxdadccaabdcbscddscc"
-FFN_TILE, FFN_ROWS, FFN_BACK = 256, 1024, 2048
+LAST_ORDER = "bxdxxbxcbdxbdcbxdbcdscbsbxcxdscbsxdcsxdccd"
+FFN_TILE, FFN_ROWS, FFN_BACK = 512, 1024, 2048
 VMEM_LIMIT = 60 * 1024 * 1024
 MODEL = 2048
 TILE = 256
@@ -114,6 +117,21 @@
     (1024, "row", 1024),
     (1024, "col", 0),
 )
+
+
+OWN_ROWS = [pltpu.VMEM((16, 8, MODEL), BF), DMA((1,))]
+
+
+def own_rows(p, ref, scratch):
+    rows, sem = scratch
+    copy = pltpu.make_async_copy(ref.at[p.x], rows, sem.at[0])
+    copy.start()
+
+    def read():
+        copy.wait()
+        return rows[...].astype(F32).reshape(BLOCK, MODEL)
+
+    return read
 
 
 class Gather:
@@ -292,6 +310,7 @@
     attn_in_t_o,
     qkv_o,
     attn_in,
+    rope_own,
     x_all,
     qkv_send,
     stage_o,
@@ -331,6 +350,10 @@
     x_out = remote(x_ref, x_all.at[:, 1], misc_send.at[0], misc_recv.at[0], p.sib())
     x_out.start()
     g.start()
+    rope_in = pltpu.make_async_copy(
+        rope_ref.at[:, pl.ds(pl.multiple_of(p.k * BLOCK, BLOCK), BLOCK)], rope_own, loc.at[4]
+    )
+    rope_in.start()
     gain_own = pltpu.make_async_copy(gain_ref, gains_o.at[p.s], loc.at[1])
     gain_own.start()
     meta_own = pltpu.make_async_copy(meta_ref, meta_o.at[p.c], loc.at[2])
@@ -361,6 +384,7 @@
         return carry
 
     lax.fori_loop(0, 8, norm_step, 0)
+    rope_in.wait()
     for i in range(4):
         g.pass_on(i)
     cot_in.wait()
@@ -396,7 +420,7 @@
             w = wqkv_o[:, :, cols].reshape(MODEL, 256)
             v = jnp.dot(a, w, preferred_element_type=F32)
             if part < 2:
-                v = v * wide(rope_ref[0]) + swap_halves(v) * wide(rope_ref[1])
+                v = v * wide(rope_own[0]) + swap_halves(v) * wide(rope_own[1])
             v = v.reshape(32, 8, 256).astype(BF)
             qkv_send[j * 2, :, :, cols] = v[:16]
             qkv_send[j * 2 + 1, :, :, cols] = v[16:]
@@ -446,7 +470,7 @@
             remote(here, here, a2a_send.at[i], a2a_recv.at[i], p.member(i)).wait_recv()
 
 
-def start_call(x, cot, weights, gains, meta, rope_own):
+def start_call(x, cot, weights, gains, meta, rope):
     shapes = (
         jax.ShapeDtypeStruct((256, 8, 768), BF),
         jax.ShapeDtypeStruct((32, 8, 2048), BF),
@@ -459,15 +483,16 @@
     return pl.pallas_call(
         start_kernel,
         out_shape=shapes,
-        in_specs=[ANY] * 6 + [VM, ANY, VM],
+        in_specs=[ANY] * 6 + [VM, ANY, ANY],
         out_specs=[VM, ANY, VM, ANY, ANY, VM, ANY],
         scratch_shapes=[
             pltpu.VMEM((4, 256, MODEL), BF),
+            pltpu.VMEM((2, BLOCK, 128), F32),
             pltpu.VMEM((4, 2, 16, 8, MODEL), BF),
             pltpu.VMEM((8, 16, 8, 768), BF),
             pltpu.VMEM((32, 8, 512), BF),
             pltpu.VMEM((4, 16, 8, MODEL), BF),
-            DMA((4,)),
+            DMA((5,)),
             DMA((3,)),
             DMA((3,)),
             DMA((3,)),
@@ -477,7 +502,7 @@
         ]
         + Gather.sems(4),
         compiler_params=params(1),
-    )(tiles(x), tiles(cot), *[tiles(w) for w in weights], gains, meta, rope_own)
+    )(tiles(x), tiles(cot), *[tiles(w) for w in weights], gains, meta, rope)
 
 
 def bias_rows(qb, rows, prow, vrow, pcol):
@@ -733,8 +758,8 @@
     "down_b": (64, 512, "col", 64, ()),
     "gate_a": (64, 512, "row", 0, (1024,)),
     "gate_b": (64, 512, "row", 512, (1024,)),
-    "up_a": (64, 512, "row", 0, (1024,)),
-    "up_b": (64, 512, "row", 512, (1024,)),
+    "up_a": (64, 512, "row", 0, (512,)),
+    "up_b": (64, 512, "row", 512, (512,)),
     "out": (32, 512, "col", 0, ()),
     "qkv": (64, 768, "row", 0, (256, 256, 256)),
 }
@@ -742,6 +767,7 @@
 DOWN_OUT = jax.ShapeDtypeStruct((2, 2, 2, 32, 8, 512), BF)
 OUT_OUT = jax.ShapeDtypeStruct((2, 1, 2, 16, 8, 512), BF)
 FFN_OUT = jax.ShapeDtypeStruct((2, 32, 8, 2048), BF)
+UP_OUT = jax.ShapeDtypeStruct((2, 32, 8, 1024), BF)
 QKV_OUT = jax.ShapeDtypeStruct((2, 32, 8, 512), BF)
 
 
@@ -864,7 +890,7 @@
     else:
         for i, width in enumerate(widths):
             take = min(cols, width)
-            spot = outs[i].at[:, :, :, pl.ds(p.c * width + first, take)]
+            spot = outs[i].at[:, :, :, pl.ds(p.c * width + (first if width > cols else 0), take)]
             piece = pl.ds(i * take, take)
             done.append(cp(15 + i, own.at[1 - p.c, :, :, :, piece], spot, p.sib()))
             done.append(pltpu.make_async_copy(own.at[p.c, :, :, :, piece], spot, loc.at[i]))
@@ -878,9 +904,9 @@
 def out_proj_kernel(
     lhs,
     rhs,
-    x_own,
     keep,
     gains,
+    x_ref,
     wg,
     wu,
     wd,
@@ -892,6 +918,8 @@
     stage_g,
     stage_u,
     stage_d,
+    x_rows,
+    x_sem,
     *scratch,
 ):
     p = Place()
@@ -905,10 +933,11 @@
         scratch[nx:],
     )
     greet(Gather.peers(p) + [p.dev(dx=1), p.dev(dx=-1)])
+    x_read = own_rows(p, x_ref, (x_rows, x_sem))
 
     def finish(attn_out):
         stat_o[...] = jnp.full((8, 128), jnp.sum(keep[:, 0:1] * attn_out * attn_out), F32)
-        resid = x_own[...].astype(F32) + attn_out
+        resid = x_read() + attn_out
         resid_o[...] = resid
         return (resid * rms(resid) * full_row(gains, 1)).astype(BF)
 
@@ -919,7 +948,7 @@
     )
 
 
-def out_proj_call(lhs, rhs, x_own, keep, gains, weights):
+def out_proj_call(lhs, rhs, keep, gains, x, weights):
     return pl.pallas_call(
         out_proj_kernel,
         out_shape=(
@@ -929,17 +958,18 @@
             jax.ShapeDtypeStruct((256, 8, 2048), BF),
             jax.ShapeDtypeStruct((128, 8, 2048), BF),
         ),
-        in_specs=[VM] * 5 + [ANY] * 3,
+        in_specs=[VM] * 4 + [ANY] * 4,
         out_specs=[VM] * 3 + [ANY] * 2,
         scratch_shapes=[
             pltpu.VMEM((64, 8, 1024), BF),
             pltpu.VMEM((64, 8, 1024), BF),
             pltpu.VMEM((128, 8, 512), BF),
         ]
+        + OWN_ROWS
         + X_SCRATCH
         + Gather.sems(3),
         compiler_params=params(3),
-    )(lhs, rhs, x_own, keep, gains, *[tiles(w) for w in weights])
+    )(lhs, rhs, keep, gains, tiles(x), *[tiles(w) for w in weights])
 
 
 def ffn_kernel(a_ref, c_ref, wg, wu, wd, h_o, gg_o, gu_o, dd_o, dg_o, du_o, a_t):
@@ -1009,16 +1039,17 @@
     )(ffn_in, cot, wgu, wgu, wd)
 
 
-MID = ("down_a", "down_b", "gate_a", "gate_b")
+MID = ("down_a", "down_b", "gate_a", "gate_b", "up_a")
 
 
 def mid_kernel(*refs):
-    gate, up, hidden, wgu, wd, dd, dgate = refs[:7]
-    wo, resid_ref, cot_own, gains, keep, qkv, info, pcol, lse, rope = refs[7:17]
-    grad_o, resid_grad_o, gain_o, final_o, stat_o, d_o, dd_o, dgate_o = refs[17:25]
-    lhs, rhs, g_out, g_in, d_out, dk, dv = refs[25:32]
-    loc, g_send, g_recv, a2a_send, a2a_recv = refs[32:37]
-    at = 37
+    gate, up, hidden, wgu, wd, dd, dgate, dup, cot_ref = refs[:9]
+    wo, resid_ref, gains, keep, qkv, info, pcol, lse, rope = refs[9:18]
+    grad_o, resid_grad_o, gain_o, final_o, stat_o, d_o, dd_o, dgate_o, dup_o = refs[18:27]
+    lhs, rhs, g_out, g_in, d_out, dk, dv = refs[27:34]
+    loc, g_send, g_recv, a2a_send, a2a_recv = refs[34:39]
+    cot_scratch = refs[39:41]
+    at = 41
     nx = len(X_SCRATCH)
     xs = refs[at : at + nx]
     at += nx
@@ -1029,6 +1060,7 @@
     each = rows // 8
     scale = HEAD_DIM**-0.5
     mine = p.slot(p.k)
+    cot_read = own_rows(p, cot_ref, cot_scratch)
 
     def fetch(n, sources):
         j = (p.x + (2, 1, 3, 0)[n]) % 4
@@ -1078,7 +1110,7 @@
         inv = rms(resid)
         normed = resid * inv
         gain_o[...] = jnp.broadcast_to(jnp.sum(g * normed, axis=0, keepdims=True), (8, MODEL))
-        grad_resid = cot_own[...].astype(F32) + norm_back(g, normed, full_row(gains, 1), inv)
+        grad_resid = cot_read() + norm_back(g, normed, full_row(gains, 1), inv)
         resid_grad_o[...] = grad_resid
         return grad_resid.astype(BF)
 
@@ -1226,14 +1258,15 @@
     x = x_phase(
         p, multiply_out, xs, final_o, False, finish_out, preparer((hidden,), wd_in)
     )
-    a, b, c, d = [
-        unit(p, name, src, (o,), scr)
-        for name, src, o, scr in zip(MID, (dd, dd, dgate, dgate), (dd_o, dd_o, dgate_o, dgate_o), us)
+    sources = (dd, dd, dgate, dgate, dup)
+    results = (dd_o, dd_o, dgate_o, dgate_o, dup_o)
+    a, b, c, d, e = [
+        unit(p, name, src, (o,), scr) for name, src, o, scr in zip(MID, sources, results, us)
     ]
-    run(MID_ORDER, m=main(), x=x, a=a, b=b, c=c, d=d)
-
-
-def mid_call(gate, up, hidden, wgu, wd, dd, dgate, wo, *rest):
+    run(MID_ORDER, m=main(), x=x, a=a, b=b, c=c, d=d, e=e)
+
+
+def mid_call(gate, up, hidden, wgu, wd, dd, dgate, dup, cot, wo, *rest):
     scratch = list(X_SCRATCH)
     for name in MID:
         scratch += unit_scratch(name)
@@ -1249,9 +1282,10 @@
             jax.ShapeDtypeStruct((8, 16, 8, 768), BF),
             DOWN_OUT,
             FFN_OUT,
+            UP_OUT,
         ),
-        in_specs=[ANY] * 7 + [VM] * 10,
-        out_specs=[VM] * 5 + [ANY] * 3,
+        in_specs=[ANY] * 9 + [VM] * 9,
+        out_specs=[VM] * 5 + [ANY] * 4,
         scratch_shapes=[
             pltpu.VMEM((2, 2, 32, 8, 1024), BF),
             pltpu.VMEM((256, 8, 2048), BF),
@@ -1266,18 +1300,28 @@
             DMA((8,)),
             DMA((8,)),
         ]
+        + OWN_ROWS
         + scratch,
         compiler_params=params(5),
-    )(*blocks, wgu, wd, tiles(dd), tiles(dgate).reshape(4, 64, 8, 1024), wo, *rest)
-
-
-LAST = ("up_a", "up_b", "out", "qkv")
+    )(
+        *blocks,
+        wgu,
+        wd,
+        tiles(dd),
+        tiles(dgate).reshape(4, 64, 8, 1024),
+        tiles(dup).reshape(4, 64, 8, 1024),
+        tiles(cot),
+        wo,
+        *rest,
+    )
+
+
+LAST = ("up_b", "out", "qkv")
 
 
 def last_kernel(
     lhs,
     rhs,
-    x_own,
     grad_resid,
     gains,
     ffn_gain,
@@ -1288,6 +1332,7 @@
     attended,
     grad_attn,
     dup,
+    x_ref,
     *refs,
 ):
     out_o, small_o, up_o, do_o = refs[:4]
@@ -1300,12 +1345,14 @@
     for _ in LAST:
         us.append(refs[at : at + UNIT_SCRATCH])
         at += UNIT_SCRATCH
-    core_in, ring_in, s_send, s_recv, do, dw = refs[at:]
+    core_in, ring_in, s_send, s_recv, do, dw = refs[at : at + 6]
+    x_scratch = refs[at + 6 :]
     p = Place()
     greet(unit_peers(p) + [p.dev(dx=1), p.dev(dx=-1), p.dev(dx=2), p.dev(dz=2)])
+    x_read = own_rows(p, x_ref, x_scratch)
 
     def finish(g):
-        v = x_own[...].astype(F32)
+        v = x_read()
         inv = rms(v)
         normed = v * inv
         few = slice(0, 128)
@@ -1364,7 +1411,7 @@
             return carry
 
         lax.fori_loop(0, 4, step, 0)
-        yield from unit(p, LAST[2], do, (do_o,), us[2])
+        yield from unit(p, LAST[1], do, (do_o,), us[1])
 
     def qkv_unit():
         def step(n, carry):
@@ -1377,24 +1424,23 @@
             return carry
 
         lax.fori_loop(0, 4, step, 0)
-        yield from unit(p, LAST[3], dw, qkv_o, us[3])
+        yield from unit(p, LAST[2], dw, qkv_o, us[2])
 
     run(
         LAST_ORDER,
         x=x_phase(p, multiplier(lhs, rhs, True), xs, out_o, False, finish),
-        a=unit(p, LAST[0], dup, (up_o,), us[0]),
-        b=unit(p, LAST[1], dup, (up_o,), us[1]),
+        b=unit(p, LAST[0], dup, (up_o,), us[0]),
         c=out_unit(),
         d=qkv_unit(),
         s=small(),
     )
 
 
-def last_call(lhs, rhs, x_own, grad_resid, gains, small_parts, attn_in_t, attended, grad_attn, dup):
+def last_call(lhs, rhs, grad_resid, gains, small_parts, attn_in_t, attended, grad_attn, dup, x):
     scratch = list(X_SCRATCH)
     for name in LAST:
         scratch += unit_scratch(name)
-    outs = [FFN_OUT, OUT_OUT, QKV_OUT, QKV_OUT, QKV_OUT]
+    outs = [UP_OUT, OUT_OUT, QKV_OUT, QKV_OUT, QKV_OUT]
     return pl.pallas_call(
         last_kernel,
         out_shape=(
@@ -1402,7 +1448,7 @@
             jax.ShapeDtypeStruct((8, MODEL), F32),
             *outs,
         ),
-        in_specs=[VM] * 12 + [ANY],
+        in_specs=[VM] * 11 + [ANY] * 2,
         out_specs=[VM] * 2 + [ANY] * len(outs),
         scratch_shapes=scratch
         + [
@@ -1412,12 +1458,12 @@
             DMA((10,)),
             pltpu.VMEM((32, 8, MODEL), BF),
             pltpu.VMEM((4, 64, 8, 768), BF),
-        ],
+        ]
+        + OWN_ROWS,
         compiler_params=params(6),
     )(
         lhs,
         rhs,
-        x_own,
         grad_resid,
         gains,
         *small_parts,
@@ -1425,7 +1471,37 @@
         attended,
         grad_attn,
         tiles(dup).reshape(4, 64, 8, 1024),
-    )
+        tiles(x),
+    )
+
+
+def results_kernel(output, grad, q, k, v, o, gate, up_a, up_b, down, *outs):
+    for src, dst in zip((output, grad, q, k, v, o, gate), outs[:7]):
+        dst[...] = src[...].astype(dst.dtype)
+    for h in (0, 1):
+        here = slice(h * 512, (h + 1) * 512)
+        outs[7][:, h * 1024 : h * 1024 + 512] = up_a[:, here].astype(F32)
+        outs[7][:, h * 1024 + 512 : (h + 1) * 1024] = up_b[:, here].astype(F32)
+    outs[8][...] = down[...].astype(F32)
+
+
+def results_call(*arrays):
+    arrays = [a.reshape(-1, a.shape[-1]) for a in arrays]
+    steps = 4
+
+    def block(shape):
+        return pl.BlockSpec((shape[0] // steps, shape[1]), lambda i: (i, 0))
+
+    types = [BF, BF] + [F32] * 7
+    shapes = [(512, 2048)] * 2 + [(512, 512)] * 4 + [(512, 2048)] * 2 + [(2048, 512)]
+    return pl.pallas_call(
+        results_kernel,
+        grid=(steps,),
+        out_shape=[jax.ShapeDtypeStruct(sh, t) for sh, t in zip(shapes, types)],
+        in_specs=[block(a.shape) for a in arrays],
+        out_specs=[block(sh) for sh in shapes],
+        compiler_params=params(),
+    )(*arrays)
 
 
 def rope_table():
@@ -1466,7 +1542,6 @@
     ctx = lax.axis_index("context")
     positions = jnp.arange(1024, dtype=jnp.int32)
     rope = jnp.asarray(rope_table())
-    rope_own = lax.dynamic_slice_in_dim(rope, ctx * BLOCK, BLOCK, 1)
     meta = jnp.concatenate([piece_index(piece_starts, piece_ids, positions), valid_mask], axis=0)
     gains_own = jnp.concatenate(
         [
@@ -1482,7 +1557,7 @@
         (q_weight, k_weight, v_weight, o_weight),
         gains_own,
         meta,
-        rope_own,
+        rope,
     )
     seq = lax.dynamic_slice(meta_all, (ctx % 2, 0, 0), (1, 8, 1024))[0]
     piece_row = lax.dynamic_slice_in_dim(seq, ctx // 2, 1, 0)
@@ -1493,13 +1568,11 @@
     cot_all = rows_of(cot_all)
     qkv = qkv.reshape(1024, 768)
     attended, lse = attend_call(qkv, info, pcol)
-    x_own = lax.dynamic_index_in_dim(inputs, x_at, 0, keepdims=False)
-    cot_own = lax.dynamic_index_in_dim(cotangent, x_at, 0, keepdims=False)
     keep_own = lax.dynamic_slice(valid_mask, (x_at, ctx * BLOCK), (1, BLOCK)).astype(F32)
     keep = jnp.broadcast_to(keep_own.reshape(BLOCK, 1), (BLOCK, 128))
     attended = attended.reshape(4, 256, 256)
     ffn_in, resid, stat_attn, wgu, wd = out_proj_call(
-        attended, wo, x_own, keep, gains, (gate_weight, up_weight, down_weight)
+        attended, wo, keep, gains, inputs, (gate_weight, up_weight, down_weight)
     )
     ffn_in = ffn_in.reshape(1024, MODEL)
     cot_rows = cot_all.reshape(1024, MODEL)
@@ -1507,7 +1580,7 @@
         ffn_in, cot_rows, rows_of(wgu), rows_of(wd)
     )
 
-    grad_attn, grad_resid, ffn_gain_part, output, stat_ffn, d_seq, sd, sgate = mid_call(
+    grad_attn, grad_resid, ffn_gain_part, output, stat_ffn, d_seq, sd, sgate, sup_a = mid_call(
         grad_gate,
         grad_up,
         hidden,
@@ -1515,9 +1588,10 @@
         wd,
         dd,
         dgate,
+        dup,
+        cotangent,
         wo,
         resid,
-        cot_own,
         gains,
         keep,
         qkv,
@@ -1527,10 +1601,9 @@
         rope,
     )
     dqkv = d_seq.reshape(4, 256, 768)
-    input_grad, small, sup, so, sq, sk, sv = last_call(
+    input_grad, small, sup_b, so, sq, sk, sv = last_call(
         dqkv,
         wqkv,
-        x_own,
         grad_resid,
         gains,
         (ffn_gain_part, stat_attn, stat_ffn, keep),
@@ -1538,8 +1611,11 @@
         attended,
         grad_attn.reshape(1024, MODEL),
         dup,
-    )
-    grads = [v.reshape(-1, v.shape[-1]).astype(F32) for v in (sq, sk, sv, so, sgate, sup, sd)]
+        inputs,
+    )
+    output, input_grad, *grads = results_call(
+        output, input_grad, sq, sk, sv, so, sgate, sup_a, sup_b, sd
+    )
     branch_rms = jnp.sqrt(small[3:6, 0] / (jnp.maximum(small[2, 0], 1.0) * MODEL))
     gain_start = (lax.axis_index("shard") * 4 + x_at) * BLOCK
     attn_gain_out = lax.dynamic_slice(small, (0, gain_start), (1, BLOCK))[0]

time: 502 us -> 473 us (0.942)
  other arithmetic: 22.5 us -> 7.61 us
  local copies, waits for them, and re-layouts: 12.8 us -> 5.24 us
  Pallas kernels: 458 us -> 452 us
    pallas_call x1, Pallas kernels: 138 us -> 110 us  [last_call(): pl.pallas_call(last_kernel, out_shape=(jax.ShapeDtypeStruct((4, 1, BLOCK,...]
    convert_element_type x7 -> x0, other arithmetic: 14.9 us -> none  [per_device(): v.reshape(-1, v.shape[-1]).astype(F32)]
    pallas_call x0 -> x1, Pallas kernels: none -> 12.3 us  [results_call(): pl.pallas_call(results_kernel, grid=(steps,), out_shape=[jax.ShapeDtypeSt...]
    pallas_call x1, Pallas kernels: 135 us -> 146 us  [mid_call(): pl.pallas_call(mid_kernel, out_shape=(jax.ShapeDtypeStruct((4, 2, BLOCK,...]
where the time goes in v1:
time: 473 us; the launch traced here: 467 us
  Pallas kernels  452 us (96%)
  other arithmetic  7.61 us (2%)
  local copies, waits for them, and re-layouts  5.24 us (1%)
    pallas_call x1, Pallas kernels, mid_call(): pl.pallas_call(mid_kernel, out_shape=(jax.ShapeDtypeStruct((4, 2, BLOCK,...  146 us
    pallas_call x1, Pallas kernels, last_call(): pl.pallas_call(last_kernel, out_shape=(jax.ShapeDtypeStruct((4, 1, BLOCK,...  110 us
    pallas_call x1, Pallas kernels, out_proj_call(): pl.pallas_call(out_proj_kernel, out_shape=(jax.ShapeDtypeStruct((4, 2, BL...  64.3 us
    pallas_call x1, Pallas kernels, start_call(): pl.pallas_call(start_kernel, out_shape=shapes, in_specs=[ANY] * 6 + [VM,...  54.6 us
    pallas_call x1, Pallas kernels, ffn_call(): pl.pallas_call(ffn_kernel, grid=(n,), out_shape=(tokens, tokens, tokens,...  39.7 us
    pallas_call x1, Pallas kernels, attend_call(): pl.pallas_call(attend_kernel, out_shape=(jax.ShapeDtypeStruct((8, 16, 8,...  24.9 us
    pallas_call x1, Pallas kernels, results_call(): pl.pallas_call(results_kernel, grid=(steps,), out_shape=[jax.ShapeDtypeSt...  12.3 us

profile of v1, /device:TPU:1, one launch (start us, length us, event | category | flops | bytes accessed | tf_op | source)
XLA Modules:
  0.0 466.9 jit_solution(13150125929263347529)
XLA Ops:
  0.7 0.8 convert_bitcast_fusion
  1.5 0.1 pad.7.clone
  1.5 0.1 pad.2.clone
  1.6 0.7 broadcast_in_dim.61
  2.3 0.7 broadcast_in_dim.62
  3.0 0.7 broadcast_add_fusion.1
  3.7 0.7 maximum_maximum_fusion.gain_ref
  4.3 0.8 select_reduce_fusion
  5.1 1.3 pad_add_fusion.meta_ref
  6.5 0.7 broadcast_in_dim.60.keep.refs_12_
  7.2 54.6 %shard_map.238 = (bf16[256,8,768]{2,1,0:T(8,128)(2,1)}, bf16[32,8,2048]{2,1,0:T(8,128)(2,1)}, f32[4,8,512]{2,1,0:T(8,128)}, s32[2,8,1024]{2,1,0:T(8,128)}, bf16[...) custom-call(bf16[4,16,8,2048]{3,2,1,0:T(8,128)(2,1)} %bitcast.52, ...), custom_call_target="tpu_custom_call" | custom-call | tf_op jit(solution)/shard_map/pallas_call | solution.py:483
  61.8 0.9 constant_dynamic-slice_fusion.1
  62.6 0.7 add_add_fusion.info.refs_14_
  63.3 1.0 broadcast_in_dim.58.pcol.refs_15_
  64.3 24.9 %shard_map.239 = (bf16[8,16,8,256]{3,2,1,0:T(8,128)(2,1)}, f32[1024,128]{1,0:T(8,128)}) custom-call(bf16[1024,768]{1,0:T(8,128)(2,1)} %bitcast.60, s32[8,1024]{1,0:T(8,128)} %add_add_fusion.info.refs_14_, s32[1024,128]{1,0:T(8,128)} %broadcast_in_dim.58.pcol.refs_15_), custom_call_target="tpu_custom_call" | custom-call | tf_op jit(solution)/shard_map/pallas_call | solution.py:581
  89.2 64.3 %shard_map.240 = (bf16[4,2,128,2048]{3,2,1,0:T(8,128)(2,1)}, f32[128,2048]{1,0:T(8,128)}, f32[8,128]{1,0:T(8,128)}, bf16[256,8,2048]{2,1,0:T(8,128)(2,1)}, bf16[128,8,2048]{2,1,0:T(8,128)(2,1)}) custom-call(bf16[4,256,256]{2,1,0:T(8,128)(2,1)} %bitcast.76, bf16[256,2048]{1,0:T(8,128)(2,1)} %bitcast.64, f32[128,128]{1,0:T(8,128)} %broadcast_in_dim.60.keep.refs_12_, ...), custom_call_target="tpu_custom_call" | custom-call | tf_op jit(solution)/shard_map/pallas_call | solution.py:952
  153.6 39.7 %shard_map.241 = (bf16[1024,1024]{1,0:T(8,128)(2,1)}, bf16[1024,1024]{1,0:T(8,128)(2,1)}, bf16[1024,1024]{1,0:T(8,128)(2,1)}, bf16[1024,2048]{1,0:T(8,128)(2,1)}...) custom-call(bf16[1024,2048]{1,0:T(8,128)(2,1)} %bitcast.63, bf16[1024,2048]{1,0:T(8,128)(2,1)} %bitcast.62, ...), custom_call_target="tpu_custom_call" | custom-call | tf_op jit(solution)/shard_map/pallas_call | solution.py:1031
  193.3 146.2 %shard_map.242 = (bf16[4,2,128,2048]{3,2,1,0:T(8,128)(2,1)}, f32[128,2048]{1,0:T(8,128)}, f32[8,2048]{1,0:T(8,128)}, bf16[4,1,128,2048]{3,2,1,0:T(8,128)(2,1)}, ...) custom-call(bf16[4,32,8,1024]{3,2,1,0:T(8,128)(2,1)} %bitcast.74, ...), custom_call_target="tpu_custom_call" | custom-call | tf_op jit(solution)/shard_map/pallas_call | solution.py:1274
  339.5 110.1 %shard_map.243 = (bf16[4,1,128,2048]{3,2,1,0:T(8,128)(2,1)}, f32[8,2048]{1,0:T(8,128)}, bf16[2,32,8,1024]{3,2,1,0:T(8,128)(2,1)}, bf16[2,1,2,16,8,512]{5,4,3,2,1...) custom-call(bf16[4,256,768]{2,1,0:T(8,128)(2,1)} %bitcast.82, ...), custom_call_target="tpu_custom_call" | custom-call | tf_op jit(solution)/shard_map/pallas_call | solution.py:1444
  449.7 1.2 slice.7
  451.5 1.3 sqrt_reduce_fusion
  452.8 1.3 dynamic-slice_bitcast_fusion.1
  454.2 12.3 %shard_map.244 = (bf16[512,2048]{1,0:T(8,128)(2,1)}, bf16[512,2048]{1,0:T(8,128)(2,1)}, f32[512,512]{1,0:T(8,128)}, f32[512,512]{1,0:T(8,128)}, f32[512,512]{1,0...) custom-call(bf16[512,2048]{1,0:T(8,128)(2,1)} %bitcast.78, ...), custom_call_target="tpu_custom_call" | custom-call | tf_op jit(solution)/shard_map/pallas_call | solution.py:1497
  (3 shorter events, 0.0 us)

commit v2 on v1

--- a/solution.py
+++ b/solution.py
@@ -299,18 +299,25 @@
     wk,
     wv,
     wo,
-    gain_ref,
-    meta_ref,
+    attn_gain,
+    ffn_gain,
+    starts,
+    ids,
+    valid,
     rope_ref,
     wqkv_o,
     wo_o,
     gains_o,
-    meta_o,
+    info_o,
+    pcol_o,
+    keep_o,
     cot_o,
     attn_in_t_o,
     qkv_o,
     attn_in,
     rope_own,
+    gain_ref,
+    meta,
     x_all,
     qkv_send,
     stage_o,
@@ -338,6 +345,9 @@
         + [p.dev(dy=dy, core=core) for dy in (-1, 1) for core in (0, 1)]
         + context_peers(p)
     )
+    gain_ref[...] = jnp.zeros_like(gain_ref)
+    gain_ref[0:1, :] = attn_gain[...].astype(F32)
+    gain_ref[1:2, :] = ffn_gain[...].astype(F32)
     gain_targets = [p.sib()] + [p.dev(dy=1, core=core) for core in (0, 1)]
     gain_copies = [
         remote(gain_ref, gains_o.at[p.s], gain_send.at[i], gain_recv.at[i if i == 0 else 1 + p.c], d)
@@ -354,19 +364,31 @@
         rope_ref.at[:, pl.ds(pl.multiple_of(p.k * BLOCK, BLOCK), BLOCK)], rope_own, loc.at[4]
     )
     rope_in.start()
-    gain_own = pltpu.make_async_copy(gain_ref, gains_o.at[p.s], loc.at[1])
-    gain_own.start()
-    meta_own = pltpu.make_async_copy(meta_ref, meta_o.at[p.c], loc.at[2])
-    meta_own.start()
-    meta_out = remote(meta_ref, meta_o.at[p.c], misc_send.at[1], misc_recv.at[1], p.sib())
+    gains_o[p.s] = gain_ref[...]
+    position = lax.broadcasted_iota(jnp.int32, (1, 1024), 1)
+    for i in range(4):
+        tag = jnp.zeros((1, 1024), jnp.int32)
+        for n in range(2):
+            first = starts[i, n]
+            inside = (position >= first) & (position < first + PIECE)
+            tag += jnp.where(inside, ids[i, n] + 1, 0)
+        meta[p.c, i : i + 1, :] = tag - 1
+    meta[p.c, 4:8, :] = valid[...]
+    meta_out = remote(meta.at[p.c], meta.at[p.c], misc_send.at[1], misc_recv.at[1], p.sib())
     meta_out.start()
+    own_row = jnp.zeros((1, 1024), jnp.int32)
+    for i in range(4):
+        own_row = jnp.where(p.x == i, valid[i : i + 1, :], own_row)
+    own_valid = own_row[:, 0:BLOCK]
+    for b in range(1, 8):
+        own_valid = jnp.where(p.k == b, own_row[:, b * BLOCK : (b + 1) * BLOCK], own_valid)
+    keep_o[...] = jnp.broadcast_to(own_valid.astype(F32), (BLOCK, BLOCK)).T
     cot_in = pltpu.make_async_copy(cot_ref, stage_cot, loc.at[3])
     cot_in.start()
     cot_own = pltpu.make_async_copy(stage_cot, cot_o.at[:, 0], loc.at[3])
     cot_out = remote(cot_ref, cot_o.at[:, 1], misc_send.at[2], misc_recv.at[2], p.sib())
     cot_out.start()
 
-    gain_own.wait()
     for i in range(3):
         block = p.yl * 2 + 1 - p.c if i == 0 else (1 - p.yl) * 2 + (i - 1)
         here = gains_o.at[block]
@@ -389,6 +411,16 @@
         g.pass_on(i)
     cot_in.wait()
     cot_own.start()
+    meta_out.wait_send()
+    here = meta.at[1 - p.c]
+    remote(here, here, misc_send.at[1], misc_recv.at[1], p.sib()).wait_recv()
+    pieces = meta[p.k % 2, pl.ds(p.k // 2, 1), :]
+    info_o[...] = jnp.zeros_like(info_o)
+    info_o[0:1, :] = pieces
+    info_o[1:2, :] = meta[p.k % 2, pl.ds(4 + p.k // 2, 1), :]
+    for b in range(8):
+        rows = slice(b * BLOCK, (b + 1) * BLOCK)
+        pcol_o[rows, :] = jnp.broadcast_to(pieces[:, rows], (BLOCK, BLOCK)).T
 
     def send_block(j, q):
         other = p.c if q == 0 else 1 - p.c
@@ -413,7 +445,8 @@
         v = jnp.concatenate([v, v], axis=1)
         return jnp.concatenate([v, v], axis=0)
 
-    def qkv_step(j, carry):
+    def qkv_step(n, carry):
+        j = (p.k // 2 + 1 + n) % 4
         a = attn_in[j]
         for part in range(3):
             cols = pl.ds(part * 256, 256)
@@ -442,10 +475,6 @@
     for i in range(4):
         g.sent(i)
     x_out.wait_send()
-    meta_own.wait()
-    meta_out.wait_send()
-    here = meta_o.at[1 - p.c]
-    remote(here, here, misc_send.at[1], misc_recv.at[1], p.sib()).wait_recv()
     cot_own.wait()
     cot_out.wait()
     for c in gain_copies:
@@ -470,12 +499,14 @@
             remote(here, here, a2a_send.at[i], a2a_recv.at[i], p.member(i)).wait_recv()
 
 
-def start_call(x, cot, weights, gains, meta, rope):
+def start_call(x, cot, weights, attn_gain, ffn_gain, starts, ids, valid, rope):
     shapes = (
         jax.ShapeDtypeStruct((256, 8, 768), BF),
         jax.ShapeDtypeStruct((32, 8, 2048), BF),
         jax.ShapeDtypeStruct((4, 8, 512), F32),
-        jax.ShapeDtypeStruct((2, 8, 1024), jnp.int32),
+        jax.ShapeDtypeStruct((8, 1024), jnp.int32),
+        jax.ShapeDtypeStruct((1024, 128), jnp.int32),
+        jax.ShapeDtypeStruct((BLOCK, BLOCK), F32),
         jax.ShapeDtypeStruct((4, 2, 16, 8, MODEL), BF),
         jax.ShapeDtypeStruct((MODEL, 1024), BF),
         jax.ShapeDtypeStruct((8, 16, 8, 768), BF),
@@ -483,11 +514,13 @@
     return pl.pallas_call(
         start_kernel,
         out_shape=shapes,
-        in_specs=[ANY] * 6 + [VM, ANY, ANY],
-        out_specs=[VM, ANY, VM, ANY, ANY, VM, ANY],
+        in_specs=[ANY] * 6 + [VM] * 2 + [pl.BlockSpec(memory_space=pltpu.SMEM)] * 2 + [VM, ANY],
+        out_specs=[VM, ANY, VM, VM, VM, VM, ANY, VM, ANY],
         scratch_shapes=[
             pltpu.VMEM((4, 256, MODEL), BF),
             pltpu.VMEM((2, BLOCK, 128), F32),
+            pltpu.VMEM((8, 512), F32),
+            pltpu.VMEM((2, 8, 1024), jnp.int32),
             pltpu.VMEM((4, 2, 16, 8, MODEL), BF),
             pltpu.VMEM((8, 16, 8, 768), BF),
             pltpu.VMEM((32, 8, 512), BF),
@@ -502,7 +535,17 @@
         ]
         + Gather.sems(4),
         compiler_params=params(1),
-    )(tiles(x), tiles(cot), *[tiles(w) for w in weights], gains, meta, rope)
+    )(
+        tiles(x),
+        tiles(cot),
+        *[tiles(w) for w in weights],
+        attn_gain[None],
+        ffn_gain[None],
+        starts,
+        ids,
+        valid,
+        rope,
+    )
 
 
 def bias_rows(qb, rows, prow, vrow, pcol):
@@ -527,7 +570,8 @@
             pltpu.make_async_copy(o_send.at[i], out_o.at[mine], a2a_send.at[i]),
         )
 
-    def step(qb, carry):
+    def step(n, carry):
+        qb = (p.k // 2 + 1 + n) % 4
         at = pl.ds(pl.multiple_of(qb * rows, rows), rows)
         bias = bias_rows(qb, rows, info[0:1, :], info[1:2, :], pcol[at, 0:1])
         lane = lax.broadcasted_iota(jnp.int32, (rows, 128), 1)
@@ -1186,7 +1230,8 @@
         for b in range(rows // BLOCK):
             d_out[qb * (rows // BLOCK) + b, :, :, 0:256] = dq[b * 16 : (b + 1) * 16]
 
-    def give(i, carry):
+    def give(n, carry):
+        i = (p.k + 1 + n) % 8
         spot = pl.ds(pl.multiple_of(i * BLOCK, BLOCK), BLOCK)
         w = dk[spot, :] * scale
         w = w * wide(rope[0, spot]) - swap_halves(w) * wide(rope[1, spot])
@@ -1475,7 +1520,16 @@
     )
 
 
-def results_kernel(output, grad, q, k, v, o, gate, up_a, up_b, down, *outs):
+def results_kernel(small, output, grad, q, k, v, o, gate, up_a, up_b, down, *outs):
+    own = pl.ds(
+        pl.multiple_of((lax.axis_index("shard") * 4 + lax.axis_index("tensor")) * BLOCK, BLOCK), BLOCK
+    )
+    outs[9][...] = small[0:1, own]
+    outs[10][...] = small[1:2, own]
+    tokens = jnp.maximum(small[2:3, 0:BLOCK], 1.0) * MODEL
+    means = [jnp.sqrt(small[i : i + 1, 0:BLOCK] / tokens) for i in (3, 4, 5)]
+    lane = lax.broadcasted_iota(jnp.int32, (1, BLOCK), 1)
+    outs[11][...] = jnp.where(lane == 0, means[0], jnp.where(lane == 1, means[1], means[2]))
     for src, dst in zip((output, grad, q, k, v, o, gate), outs[:7]):
         dst[...] = src[...].astype(dst.dtype)
     for h in (0, 1):
@@ -1485,7 +1539,7 @@
     outs[8][...] = down[...].astype(F32)
 
 
-def results_call(*arrays):
+def results_call(small, *arrays):
     arrays = [a.reshape(-1, a.shape[-1]) for a in arrays]
     steps = 4
 
@@ -1497,11 +1551,12 @@
     return pl.pallas_call(
         results_kernel,
         grid=(steps,),
-        out_shape=[jax.ShapeDtypeStruct(sh, t) for sh, t in zip(shapes, types)],
-        in_specs=[block(a.shape) for a in arrays],
-        out_specs=[block(sh) for sh in shapes],
+        out_shape=[jax.ShapeDtypeStruct(sh, t) for sh, t in zip(shapes, types)]
+        + [jax.ShapeDtypeStruct((1, BLOCK), F32)] * 3,
+        in_specs=[pl.BlockSpec((8, MODEL), lambda i: (0, 0))] + [block(a.shape) for a in arrays],
+        out_specs=[block(sh) for sh in shapes] + [pl.BlockSpec((1, BLOCK), lambda i: (0, 0))] * 3,
         compiler_params=params(),
-    )(*arrays)
+    )(small, *arrays)
 
 
 def rope_table():
@@ -1512,14 +1567,6 @@
     cosine = np.concatenate([cosine, cosine], axis=1)
     sine = np.concatenate([-sine, sine], axis=1)
     return np.stack([np.tile(cosine, (1, 2)), np.tile(sine, (1, 2))]).astype(np.float32)
-
-
-def piece_index(starts, piece_tags, positions):
-    inside = (positions[None, :, None] >= starts[:, None, :]) & (
-        positions[None, :, None] < starts[:, None, :] + PIECE
-    )
-    tagged = jnp.where(inside, piece_tags[:, None, :] + 1, 0)
-    return jnp.sum(tagged, axis=2) - 1
 
 
 def per_device(
@@ -1538,38 +1585,22 @@
     piece_ids,
     valid_mask,
 ):
-    x_at = lax.axis_index("tensor")
-    ctx = lax.axis_index("context")
-    positions = jnp.arange(1024, dtype=jnp.int32)
     rope = jnp.asarray(rope_table())
-    meta = jnp.concatenate([piece_index(piece_starts, piece_ids, positions), valid_mask], axis=0)
-    gains_own = jnp.concatenate(
-        [
-            attn_gain.astype(F32)[None],
-            ffn_gain.astype(F32)[None],
-            jnp.zeros((6, attn_gain.shape[0]), F32),
-        ],
-        axis=0,
-    )
-    wqkv, wo, gains, meta_all, cot_all, attn_in_t, qkv = start_call(
+    wqkv, wo, gains, info, pcol, keep, cot_all, attn_in_t, qkv = start_call(
         inputs,
         cotangent,
         (q_weight, k_weight, v_weight, o_weight),
-        gains_own,
-        meta,
+        attn_gain,
+        ffn_gain,
+        piece_starts,
+        piece_ids,
+        valid_mask,
         rope,
     )
-    seq = lax.dynamic_slice(meta_all, (ctx % 2, 0, 0), (1, 8, 1024))[0]
-    piece_row = lax.dynamic_slice_in_dim(seq, ctx // 2, 1, 0)
-    valid_row = lax.dynamic_slice_in_dim(seq, 4 + ctx // 2, 1, 0)
-    info = jnp.concatenate([piece_row, valid_row, jnp.zeros((6, 1024), jnp.int32)], axis=0)
-    pcol = jnp.broadcast_to(piece_row.reshape(1024, 1), (1024, 128))
     wqkv, wo = rows_of(wqkv), rows_of(wo)
     cot_all = rows_of(cot_all)
     qkv = qkv.reshape(1024, 768)
     attended, lse = attend_call(qkv, info, pcol)
-    keep_own = lax.dynamic_slice(valid_mask, (x_at, ctx * BLOCK), (1, BLOCK)).astype(F32)
-    keep = jnp.broadcast_to(keep_own.reshape(BLOCK, 1), (BLOCK, 128))
     attended = attended.reshape(4, 256, 256)
     ffn_in, resid, stat_attn, wgu, wd = out_proj_call(
         attended, wo, keep, gains, inputs, (gate_weight, up_weight, down_weight)
@@ -1613,20 +1644,16 @@
         dup,
         inputs,
     )
-    output, input_grad, *grads = results_call(
-        output, input_grad, sq, sk, sv, so, sgate, sup_a, sup_b, sd
-    )
-    branch_rms = jnp.sqrt(small[3:6, 0] / (jnp.maximum(small[2, 0], 1.0) * MODEL))
-    gain_start = (lax.axis_index("shard") * 4 + x_at) * BLOCK
-    attn_gain_out = lax.dynamic_slice(small, (0, gain_start), (1, BLOCK))[0]
-    ffn_gain_out = lax.dynamic_slice(small, (1, gain_start), (1, BLOCK))[0]
+    output, input_grad, *grads, attn_gain_out, ffn_gain_out, means = results_call(
+        small, output, input_grad, sq, sk, sv, so, sgate, sup_a, sup_b, sd
+    )
     return (
         output.reshape(4, BLOCK, MODEL),
         input_grad.reshape(4, BLOCK, MODEL),
         *grads,
-        attn_gain_out,
-        ffn_gain_out,
-        branch_rms,
+        attn_gain_out[0],
+        ffn_gain_out[0],
+        means[0, 0:3],
     )
 
 

time: 473 us -> 474 us (level)
  Pallas kernels: 452 us -> 460 us
  other arithmetic: 7.61 us -> 0 us
    pallas_call x1, Pallas kernels: 110 us -> 120 us  [last_call(): pl.pallas_call(last_kernel, out_shape=(jax.ShapeDtypeStruct((4, 1, BLOCK,...]
where the time goes in v2:
time: 474 us; the launch traced here: 468 us
  Pallas kernels  460 us (97%)
  local copies, waits for them, and re-layouts  6.38 us (1%)
    pallas_call x1, Pallas kernels, mid_call(): pl.pallas_call(mid_kernel, out_shape=(jax.ShapeDtypeStruct((4, 2, BLOCK,...  149 us
    pallas_call x1, Pallas kernels, last_call(): pl.pallas_call(last_kernel, out_shape=(jax.ShapeDtypeStruct((4, 1, BLOCK,...  120 us
    pallas_call x1, Pallas kernels, out_proj_call(): pl.pallas_call(out_proj_kernel, out_shape=(jax.ShapeDtypeStruct((4, 2, BL...  61.2 us
    pallas_call x1, Pallas kernels, start_call(): pl.pallas_call(start_kernel, out_shape=shapes, in_specs=[ANY] * 6 + [VM]...  54.4 us
    pallas_call x1, Pallas kernels, ffn_call(): pl.pallas_call(ffn_kernel, grid=(n,), out_shape=(tokens, tokens, tokens,...  39.7 us
    pallas_call x1, Pallas kernels, attend_call(): pl.pallas_call(attend_kernel, out_shape=(jax.ShapeDtypeStruct((8, 16, 8,...  23.7 us
    pallas_call x1, Pallas kernels, results_call(): pl.pallas_call(results_kernel, grid=(steps,), out_shape=[jax.ShapeDtypeSt...  12.7 us

profile of v2, /device:TPU:1, one launch (start us, length us, event | category | flops | bytes accessed | tf_op | source)
XLA Modules:
  0.0 467.6 jit_solution(11862071566300154961)
XLA Ops:
  0.6 1.3 broadcast_in_dim.6.attn_gain
  1.9 1.3 broadcast_in_dim.7.ffn_gain
  3.2 1.3 copy.27.starts
  4.5 1.3 copy.28.ids
  5.8 54.4 %shard_map.238 = (bf16[256,8,768]{2,1,0:T(8,128)(2,1)}, bf16[32,8,2048]{2,1,0:T(8,128)(2,1)}, f32[4,8,512]{2,1,0:T(8,128)}, s32[8,1024]{1,0:T(8,128)}, s32[1024,...) custom-call(bf16[4,16,8,2048]{3,2,1,0:T(8,128)(2,1)} %bitcast.43, ...), custom_call_target="tpu_custom_call" | custom-call | tf_op jit(solution)/shard_map/pallas_call | solution.py:514
  60.2 23.7 %shard_map.239 = (bf16[8,16,8,256]{3,2,1,0:T(8,128)(2,1)}, f32[1024,128]{1,0:T(8,128)}) custom-call(bf16[1024,768]{1,0:T(8,128)(2,1)} %bitcast.51, s32[8,1024]{1,0:T(8,128)} %get-tuple-element.63.info.refs_14_, s32[1024,128]{1,0:T(8,128)} %get-tuple-element.64.pcol.refs_15_), custom_call_target="tpu_custom_call" | custom-call | tf_op jit(solution)/shard_map/pallas_call | solution.py:625
  84.0 61.2 %shard_map.240 = (bf16[4,2,128,2048]{3,2,1,0:T(8,128)(2,1)}, f32[128,2048]{1,0:T(8,128)}, f32[8,128]{1,0:T(8,128)}, bf16[256,8,2048]{2,1,0:T(8,128)(2,1)}, bf16[128,8,2048]{2,1,0:T(8,128)(2,1)}) custom-call(bf16[4,256,256]{2,1,0:T(8,128)(2,1)} %bitcast.67, bf16[256,2048]{1,0:T(8,128)(2,1)} %bitcast.55, f32[128,128]{1,0:T(8,128)} %get-tuple-element.67.keep.refs_12_, ...), custom_call_target="tpu_custom_call" | custom-call | tf_op jit(solution)/shard_map/pallas_call | solution.py:996
  145.1 39.7 %shard_map.241 = (bf16[1024,1024]{1,0:T(8,128)(2,1)}, bf16[1024,1024]{1,0:T(8,128)(2,1)}, bf16[1024,1024]{1,0:T(8,128)(2,1)}, bf16[1024,2048]{1,0:T(8,128)(2,1)}...) custom-call(bf16[1024,2048]{1,0:T(8,128)(2,1)} %bitcast.54, bf16[1024,2048]{1,0:T(8,128)(2,1)} %bitcast.53, ...), custom_call_target="tpu_custom_call" | custom-call | tf_op jit(solution)/shard_map/pallas_call | solution.py:1075
  184.8 148.7 %shard_map.242 = (bf16[4,2,128,2048]{3,2,1,0:T(8,128)(2,1)}, f32[128,2048]{1,0:T(8,128)}, f32[8,2048]{1,0:T(8,128)}, bf16[4,1,128,2048]{3,2,1,0:T(8,128)(2,1)}, ...) custom-call(bf16[4,32,8,1024]{3,2,1,0:T(8,128)(2,1)} %bitcast.65, ...), custom_call_target="tpu_custom_call" | custom-call | tf_op jit(solution)/shard_map/pallas_call | solution.py:1319
  333.5 119.7 %shard_map.243 = (bf16[4,1,128,2048]{3,2,1,0:T(8,128)(2,1)}, f32[8,2048]{1,0:T(8,128)}, bf16[2,32,8,1024]{3,2,1,0:T(8,128)(2,1)}, bf16[2,1,2,16,8,512]{5,4,3,2,1...) custom-call(bf16[4,256,768]{2,1,0:T(8,128)(2,1)} %bitcast.73, ...), custom_call_target="tpu_custom_call" | custom-call | tf_op jit(solution)/shard_map/pallas_call | solution.py:1489
  453.3 12.7 %shard_map.244 = (bf16[512,2048]{1,0:T(8,128)(2,1)}, bf16[512,2048]{1,0:T(8,128)(2,1)}, f32[512,512]{1,0:T(8,128)}, f32[512,512]{1,0:T(8,128)}, f32[512,512]{1,0...) custom-call(f32[8,2048]{1,0:T(8,128)} %get-tuple-element.89.small, ...), custom_call_target="tpu_custom_call" | custom-call | tf_op jit(solution)/shard_map/pallas_call | solution.py:1551
  466.0 1.2 slice_bitcast_fusion

commit v3 on v2

--- a/solution.py
+++ b/solution.py
@@ -20,8 +20,8 @@
 DMA = pltpu.SemaphoreType.DMA
 PROJ_ORDER = "gxxxxxggxgxgxgxggx"
 MID_ORDER = (
-    "amemmcbmmaemadcemmbacmebmxcxdbaxdmeaxxdcmbe"
-    "mcxdbmdmxcabdxecxabdmexdxmbcamme"
+    "amecmmmbmaemaemdcambemcbmxcdxxdambedcmx"
+    "bxambdcexmdmxbacdeaxcxbdmdmmcbxxaeem"
 )
 ATTEND_ROWS = 256
 LAST_ORDER = "bxdxxbxcbdxbdcbxdbcdscbsbxcxdscbsxdcsxdccd"
@@ -301,8 +301,7 @@
     wo,
     attn_gain,
     ffn_gain,
-    starts,
-    ids,
+    pieces_ref,
     valid,
     rope_ref,
     wqkv_o,
@@ -369,9 +368,9 @@
     for i in range(4):
         tag = jnp.zeros((1, 1024), jnp.int32)
         for n in range(2):
-            first = starts[i, n]
+            first = pieces_ref[i, n]
             inside = (position >= first) & (position < first + PIECE)
-            tag += jnp.where(inside, ids[i, n] + 1, 0)
+            tag += jnp.where(inside, pieces_ref[i, 2 + n] + 1, 0)
         meta[p.c, i : i + 1, :] = tag - 1
     meta[p.c, 4:8, :] = valid[...]
     meta_out = remote(meta.at[p.c], meta.at[p.c], misc_send.at[1], misc_recv.at[1], p.sib())
@@ -514,7 +513,7 @@
     return pl.pallas_call(
         start_kernel,
         out_shape=shapes,
-        in_specs=[ANY] * 6 + [VM] * 2 + [pl.BlockSpec(memory_space=pltpu.SMEM)] * 2 + [VM, ANY],
+        in_specs=[ANY] * 6 + [VM] * 2 + [pl.BlockSpec(memory_space=pltpu.SMEM), VM, ANY],
         out_specs=[VM, ANY, VM, VM, VM, VM, ANY, VM, ANY],
         scratch_shapes=[
             pltpu.VMEM((4, 256, MODEL), BF),
@@ -541,8 +540,7 @@
         *[tiles(w) for w in weights],
         attn_gain[None],
         ffn_gain[None],
-        starts,
-        ids,
+        jnp.concatenate([starts, ids], axis=1),
         valid,
         rope,
     )
@@ -807,7 +805,7 @@
     "out": (32, 512, "col", 0, ()),
     "qkv": (64, 768, "row", 0, (256, 256, 256)),
 }
-UNIT_SCRATCH = 8
+UNIT_SCRATCH = 9
 DOWN_OUT = jax.ShapeDtypeStruct((2, 2, 2, 32, 8, 512), BF)
 OUT_OUT = jax.ShapeDtypeStruct((2, 1, 2, 16, 8, 512), BF)
 FFN_OUT = jax.ShapeDtypeStruct((2, 32, 8, 2048), BF)
@@ -826,6 +824,7 @@
         DMA((4,)),
         DMA((18,)),
         DMA((18,)),
+        pltpu.SemaphoreType.REGULAR,
     ]
 
 
@@ -833,9 +832,9 @@
     return [p.sib(), p.dev(dy=1), p.dev(dy=-1), p.dev(dy=2), p.dev(dz=1), p.dev(dz=-1)]
 
 
-def unit(p, name, src, outs, scratch):
+def unit(p, name, src, outs, scratch, pace=False):
     rows, cols, kind, first, widths = UNITS[name]
-    own, yin, zout, zin, yhin, loc, send, recv = scratch
+    own, yin, zout, zin, yhin, loc, send, recv, beside = scratch
     part = rows // 8
     half = rows // 2
     z_of = {0: p.dev(dz=1), 1: p.dev(dz=-1)}
@@ -874,7 +873,7 @@
         c.wait()
     for c in along_y:
         c.wait_recv()
-    own[...] = (own[...].astype(F32) + yin[...].astype(F32)).astype(BF)
+    own[...] = own[...] + yin[...]
 
     def chunk(h, zc):
         return own.at[:, h, pl.ds(zc * part, part)]
@@ -889,9 +888,7 @@
     for side, zc in ((0, zr), (1, zl)):
         zout[side, :, 1 - side] = own[:, 1 - side, pl.ds(zc * part, part)]
         far[side].wait_recv()
-        zout[side, :, side] = (
-            own[:, side, pl.ds(zc * part, part)].astype(F32) + zin[0, :, side].astype(F32)
-        ).astype(BF)
+        zout[side, :, side] = own[:, side, pl.ds(zc * part, part)] + zin[0, :, side]
         c = cp(6 + side, zout.at[side], zin.at[1 + side], z_of[side])
         c.start()
         near.append(c)
@@ -902,11 +899,15 @@
         c.wait_send()
     v = own[:, :, pl.ds(me * part, part)].astype(F32)
     zout[0] = (v + zin[1].astype(F32) + zin[2].astype(F32)).astype(BF)
+    if pace:
+        for dy in (-1, 1):
+            pl.semaphore_signal(beside, inc=1, device_id=p.dev(dy=dy), device_id_type=MESH_ID)
+        pl.semaphore_wait(beside, 2)
     yh = cp(8, zout.at[0], yhin, p.dev(dy=2))
     yh.start()
     yield
     yh.wait_recv()
-    own[:, :, pl.ds(me * part, part)] = (zout[0].astype(F32) + yhin[...].astype(F32)).astype(BF)
+    own[:, :, pl.ds(me * part, part)] = zout[0] + yhin[...]
     back = [cp(9 + side * 2 + h, chunk(h, me), chunk(h, me), z_of[side]) for side, h in ((0, 0), (1, 1), (0, 1), (1, 0))]
     for c in back:
         c.start()
@@ -1230,8 +1231,7 @@
         for b in range(rows // BLOCK):
             d_out[qb * (rows // BLOCK) + b, :, :, 0:256] = dq[b * 16 : (b + 1) * 16]
 
-    def give(n, carry):
-        i = (p.k + 1 + n) % 8
+    def give(i, carry):
         spot = pl.ds(pl.multiple_of(i * BLOCK, BLOCK), BLOCK)
         w = dk[spot, :] * scale
         w = w * wide(rope[0, spot]) - swap_halves(w) * wide(rope[1, spot])
@@ -1306,7 +1306,8 @@
     sources = (dd, dd, dgate, dgate, dup)
     results = (dd_o, dd_o, dgate_o, dgate_o, dup_o)
     a, b, c, d, e = [
-        unit(p, name, src, (o,), scr) for name, src, o, scr in zip(MID, sources, results, us)
+        unit(p, name, src, (o,), scr, True)
+        for name, src, o, scr in zip(MID, sources, results, us)
     ]
     run(MID_ORDER, m=main(), x=x, a=a, b=b, c=c, d=d, e=e)
 

time: 474 us -> 459 us (0.968)
  Pallas kernels: 460 us -> 446 us
    pallas_call x1, Pallas kernels: 120 us -> 94.4 us  [last_call(): pl.pallas_call(last_kernel, out_shape=(jax.ShapeDtypeStruct((4, 1, BLOCK,...]
    pallas_call x1, Pallas kernels: 149 us -> 160 us  [mid_call(): pl.pallas_call(mid_kernel, out_shape=(jax.ShapeDtypeStruct((4, 2, BLOCK,...]
where the time goes in v3:
time: 459 us; the launch traced here: 452 us
  Pallas kernels  446 us (97%)
  local copies, waits for them, and re-layouts  5.24 us (1%)
    pallas_call x1, Pallas kernels, mid_call(): pl.pallas_call(mid_kernel, out_shape=(jax.ShapeDtypeStruct((4, 2, BLOCK,...  160 us
    pallas_call x1, Pallas kernels, last_call(): pl.pallas_call(last_kernel, out_shape=(jax.ShapeDtypeStruct((4, 1, BLOCK,...  94.4 us
    pallas_call x1, Pallas kernels, out_proj_call(): pl.pallas_call(out_proj_kernel, out_shape=(jax.ShapeDtypeStruct((4, 2, BL...  61.2 us
    pallas_call x1, Pallas kernels, start_call(): pl.pallas_call(start_kernel, out_shape=shapes, in_specs=[ANY] * 6 + [VM]...  54.3 us
    pallas_call x1, Pallas kernels, ffn_call(): pl.pallas_call(ffn_kernel, grid=(n,), out_shape=(tokens, tokens, tokens,...  39.5 us
    pallas_call x1, Pallas kernels, attend_call(): pl.pallas_call(attend_kernel, out_shape=(jax.ShapeDtypeStruct((8, 16, 8,...  23.8 us
    pallas_call x1, Pallas kernels, results_call(): pl.pallas_call(results_kernel, grid=(steps,), out_shape=[jax.ShapeDtypeSt...  12.7 us

profile of v3, /device:TPU:1, one launch (start us, length us, event | category | flops | bytes accessed | tf_op | source)
XLA Modules:
  0.0 452.5 jit_solution(2375558181300133123)
XLA Ops:
  0.6 1.3 broadcast_in_dim.6.attn_gain
  1.9 1.3 broadcast_in_dim.7.ffn_gain
  3.2 0.8 copy.27
  3.9 0.8 copy.28
  4.7 0.7 pad_add_fusion.pieces_ref
  5.3 54.3 %shard_map.238 = (bf16[256,8,768]{2,1,0:T(8,128)(2,1)}, bf16[32,8,2048]{2,1,0:T(8,128)(2,1)}, f32[4,8,512]{2,1,0:T(8,128)}, s32[8,1024]{1,0:T(8,128)}, s32[1024,...) custom-call(bf16[4,16,8,2048]{3,2,1,0:T(8,128)(2,1)} %bitcast.43, ...), custom_call_target="tpu_custom_call" | custom-call | tf_op jit(solution)/shard_map/pallas_call | solution.py:513
  59.7 23.8 %shard_map.239 = (bf16[8,16,8,256]{3,2,1,0:T(8,128)(2,1)}, f32[1024,128]{1,0:T(8,128)}) custom-call(bf16[1024,768]{1,0:T(8,128)(2,1)} %bitcast.51, s32[8,1024]{1,0:T(8,128)} %get-tuple-element.63.info.refs_14_, s32[1024,128]{1,0:T(8,128)} %get-tuple-element.64.pcol.refs_15_), custom_call_target="tpu_custom_call" | custom-call | tf_op jit(solution)/shard_map/pallas_call | solution.py:623
  83.4 61.2 %shard_map.240 = (bf16[4,2,128,2048]{3,2,1,0:T(8,128)(2,1)}, f32[128,2048]{1,0:T(8,128)}, f32[8,128]{1,0:T(8,128)}, bf16[256,8,2048]{2,1,0:T(8,128)(2,1)}, bf16[128,8,2048]{2,1,0:T(8,128)(2,1)}) custom-call(bf16[4,256,256]{2,1,0:T(8,128)(2,1)} %bitcast.67, bf16[256,2048]{1,0:T(8,128)(2,1)} %bitcast.55, f32[128,128]{1,0:T(8,128)} %get-tuple-element.67.keep.refs_12_, ...), custom_call_target="tpu_custom_call" | custom-call | tf_op jit(solution)/shard_map/pallas_call | solution.py:997
  144.6 39.5 %shard_map.241 = (bf16[1024,1024]{1,0:T(8,128)(2,1)}, bf16[1024,1024]{1,0:T(8,128)(2,1)}, bf16[1024,1024]{1,0:T(8,128)(2,1)}, bf16[1024,2048]{1,0:T(8,128)(2,1)}...) custom-call(bf16[1024,2048]{1,0:T(8,128)(2,1)} %bitcast.54, bf16[1024,2048]{1,0:T(8,128)(2,1)} %bitcast.53, ...), custom_call_target="tpu_custom_call" | custom-call | tf_op jit(solution)/shard_map/pallas_call | solution.py:1076
  184.1 159.9 %shard_map.242 = (bf16[4,2,128,2048]{3,2,1,0:T(8,128)(2,1)}, f32[128,2048]{1,0:T(8,128)}, f32[8,2048]{1,0:T(8,128)}, bf16[4,1,128,2048]{3,2,1,0:T(8,128)(2,1)}, ...) custom-call(bf16[4,32,8,1024]{3,2,1,0:T(8,128)(2,1)} %bitcast.65, ...), custom_call_target="tpu_custom_call" | custom-call | tf_op jit(solution)/shard_map/pallas_call | solution.py:1320
  344.0 94.4 %shard_map.243 = (bf16[4,1,128,2048]{3,2,1,0:T(8,128)(2,1)}, f32[8,2048]{1,0:T(8,128)}, bf16[2,32,8,1024]{3,2,1,0:T(8,128)(2,1)}, bf16[2,1,2,16,8,512]{5,4,3,2,1...) custom-call(bf16[4,256,768]{2,1,0:T(8,128)(2,1)} %bitcast.73, ...), custom_call_target="tpu_custom_call" | custom-call | tf_op jit(solution)/shard_map/pallas_call | solution.py:1490
  438.4 12.7 %shard_map.244 = (bf16[512,2048]{1,0:T(8,128)(2,1)}, bf16[512,2048]{1,0:T(8,128)(2,1)}, f32[512,512]{1,0:T(8,128)}, f32[512,512]{1,0:T(8,128)}, f32[512,512]{1,0...) custom-call(f32[8,2048]{1,0:T(8,128)} %get-tuple-element.89.small, ...), custom_call_target="tpu_custom_call" | custom-call | tf_op jit(solution)/shard_map/pallas_call | solution.py:1552
  451.1 1.2 slice_bitcast_fusion

commit v4 on v3

--- a/solution.py
+++ b/solution.py
@@ -299,8 +299,7 @@
     wk,
     wv,
     wo,
-    attn_gain,
-    ffn_gain,
+    gains_ref,
     pieces_ref,
     valid,
     rope_ref,
@@ -345,8 +344,7 @@
         + context_peers(p)
     )
     gain_ref[...] = jnp.zeros_like(gain_ref)
-    gain_ref[0:1, :] = attn_gain[...].astype(F32)
-    gain_ref[1:2, :] = ffn_gain[...].astype(F32)
+    gain_ref[0:2, :] = gains_ref[...]
     gain_targets = [p.sib()] + [p.dev(dy=1, core=core) for core in (0, 1)]
     gain_copies = [
         remote(gain_ref, gains_o.at[p.s], gain_send.at[i], gain_recv.at[i if i == 0 else 1 + p.c], d)
@@ -401,26 +399,18 @@
         r = lax.rsqrt(jnp.mean(v * v, axis=1, keepdims=True) + NORM_EPS)
         v = (v * r * gain).astype(BF)
         attn_in[i // 2, pl.ds((i % 2) * BLOCK, BLOCK), :] = v
-        attn_in_t_o[:, pl.ds(pl.multiple_of(i * BLOCK, BLOCK), BLOCK)] = v.T
         return carry
 
-    lax.fori_loop(0, 8, norm_step, 0)
+    lax.fori_loop(0, 3, norm_step, 0)
+    g.pass_on(0)
+    lax.fori_loop(3, 6, norm_step, 0)
+    g.pass_on(1)
+    lax.fori_loop(6, 8, norm_step, 0)
+    g.pass_on(2)
+    g.pass_on(3)
     rope_in.wait()
-    for i in range(4):
-        g.pass_on(i)
     cot_in.wait()
     cot_own.start()
-    meta_out.wait_send()
-    here = meta.at[1 - p.c]
-    remote(here, here, misc_send.at[1], misc_recv.at[1], p.sib()).wait_recv()
-    pieces = meta[p.k % 2, pl.ds(p.k // 2, 1), :]
-    info_o[...] = jnp.zeros_like(info_o)
-    info_o[0:1, :] = pieces
-    info_o[1:2, :] = meta[p.k % 2, pl.ds(4 + p.k // 2, 1), :]
-    for b in range(8):
-        rows = slice(b * BLOCK, (b + 1) * BLOCK)
-        pcol_o[rows, :] = jnp.broadcast_to(pieces[:, rows], (BLOCK, BLOCK)).T
-
     def send_block(j, q):
         other = p.c if q == 0 else 1 - p.c
         k = j * 2 + other
@@ -470,6 +460,23 @@
         return carry
 
     lax.fori_loop(0, 4, qkv_step, 0)
+
+    def turn_step(i, carry):
+        cols = pl.ds(pl.multiple_of(i * 256, 256), 256)
+        attn_in_t_o[:, cols] = attn_in[i].T
+        return carry
+
+    lax.fori_loop(0, 4, turn_step, 0)
+    meta_out.wait_send()
+    here = meta.at[1 - p.c]
+    remote(here, here, misc_send.at[1], misc_recv.at[1], p.sib()).wait_recv()
+    pieces = meta[p.k % 2, pl.ds(p.k // 2, 1), :]
+    info_o[...] = jnp.zeros_like(info_o)
+    info_o[0:1, :] = pieces
+    info_o[1:2, :] = meta[p.k % 2, pl.ds(4 + p.k // 2, 1), :]
+    for b in range(8):
+        rows = slice(b * BLOCK, (b + 1) * BLOCK)
+        pcol_o[rows, :] = jnp.broadcast_to(pieces[:, rows], (BLOCK, BLOCK)).T
     g.arrive(3)
     for i in range(4):
         g.sent(i)
@@ -513,7 +520,7 @@
     return pl.pallas_call(
         start_kernel,
         out_shape=shapes,
-        in_specs=[ANY] * 6 + [VM] * 2 + [pl.BlockSpec(memory_space=pltpu.SMEM), VM, ANY],
+        in_specs=[ANY] * 6 + [VM] + [pl.BlockSpec(memory_space=pltpu.SMEM), VM, ANY],
         out_specs=[VM, ANY, VM, VM, VM, VM, ANY, VM, ANY],
         scratch_shapes=[
             pltpu.VMEM((4, 256, MODEL), BF),
@@ -538,8 +545,7 @@
         tiles(x),
         tiles(cot),
         *[tiles(w) for w in weights],
-        attn_gain[None],
-        ffn_gain[None],
+        jnp.stack([attn_gain, ffn_gain]).astype(F32),
         jnp.concatenate([starts, ids], axis=1),
         valid,
         rope,

time: 459 us -> 456 us (level)
  no operation moved by 1% of the time
where the time goes in v4:
time: 456 us; the launch traced here: 449 us
  Pallas kernels  443 us (97%)
    pallas_call x1, Pallas kernels, mid_call(): pl.pallas_call(mid_kernel, out_shape=(jax.ShapeDtypeStruct((4, 2, BLOCK,...  160 us
    pallas_call x1, Pallas kernels, last_call(): pl.pallas_call(last_kernel, out_shape=(jax.ShapeDtypeStruct((4, 1, BLOCK,...  94.4 us
    pallas_call x1, Pallas kernels, out_proj_call(): pl.pallas_call(out_proj_kernel, out_shape=(jax.ShapeDtypeStruct((4, 2, BL...  61 us
    pallas_call x1, Pallas kernels, start_call(): pl.pallas_call(start_kernel, out_shape=shapes, in_specs=[ANY] * 6 + [VM]...  51.5 us
    pallas_call x1, Pallas kernels, ffn_call(): pl.pallas_call(ffn_kernel, grid=(n,), out_shape=(tokens, tokens, tokens,...  39.4 us
    pallas_call x1, Pallas kernels, attend_call(): pl.pallas_call(attend_kernel, out_shape=(jax.ShapeDtypeStruct((8, 16, 8,...  23.7 us
    pallas_call x1, Pallas kernels, results_call(): pl.pallas_call(results_kernel, grid=(steps,), out_shape=[jax.ShapeDtypeSt...  12.7 us

profile of v4, /device:TPU:1, one launch (start us, length us, event | category | flops | bytes accessed | tf_op | source)
XLA Modules:
  0.0 448.9 jit_solution(8989815914625488909)
XLA Ops:
  0.6 0.7 stack.9
  1.3 0.7 stack.10
  2.0 0.6 maximum_convert_fusion.gains_ref
  2.6 0.8 copy.27
  3.4 0.8 copy.28
  4.1 0.7 pad_add_fusion.pieces_ref
  4.8 51.5 %shard_map.238 = (bf16[256,8,768]{2,1,0:T(8,128)(2,1)}, bf16[32,8,2048]{2,1,0:T(8,128)(2,1)}, f32[4,8,512]{2,1,0:T(8,128)}, s32[8,1024]{1,0:T(8,128)}, s32[1024,...) custom-call(bf16[4,16,8,2048]{3,2,1,0:T(8,128)(2,1)} %bitcast.43, ...), custom_call_target="tpu_custom_call" | custom-call | tf_op jit(solution)/shard_map/pallas_call | solution.py:520
  56.3 23.7 %shard_map.239 = (bf16[8,16,8,256]{3,2,1,0:T(8,128)(2,1)}, f32[1024,128]{1,0:T(8,128)}) custom-call(bf16[1024,768]{1,0:T(8,128)(2,1)} %bitcast.51, s32[8,1024]{1,0:T(8,128)} %get-tuple-element.63.info.refs_14_, s32[1024,128]{1,0:T(8,128)} %get-tuple-element.64.pcol.refs_15_), custom_call_target="tpu_custom_call" | custom-call | tf_op jit(solution)/shard_map/pallas_call | solution.py:629
  80.1 61.0 %shard_map.240 = (bf16[4,2,128,2048]{3,2,1,0:T(8,128)(2,1)}, f32[128,2048]{1,0:T(8,128)}, f32[8,128]{1,0:T(8,128)}, bf16[256,8,2048]{2,1,0:T(8,128)(2,1)}, bf16[128,8,2048]{2,1,0:T(8,128)(2,1)}) custom-call(bf16[4,256,256]{2,1,0:T(8,128)(2,1)} %bitcast.67, bf16[256,2048]{1,0:T(8,128)(2,1)} %bitcast.55, f32[128,128]{1,0:T(8,128)} %get-tuple-element.67.keep.refs_12_, ...), custom_call_target="tpu_custom_call" | custom-call | tf_op jit(solution)/shard_map/pallas_call | solution.py:1003
  141.1 39.4 %shard_map.241 = (bf16[1024,1024]{1,0:T(8,128)(2,1)}, bf16[1024,1024]{1,0:T(8,128)(2,1)}, bf16[1024,1024]{1,0:T(8,128)(2,1)}, bf16[1024,2048]{1,0:T(8,128)(2,1)}...) custom-call(bf16[1024,2048]{1,0:T(8,128)(2,1)} %bitcast.54, bf16[1024,2048]{1,0:T(8,128)(2,1)} %bitcast.53, ...), custom_call_target="tpu_custom_call" | custom-call | tf_op jit(solution)/shard_map/pallas_call | solution.py:1082
  180.6 159.9 %shard_map.242 = (bf16[4,2,128,2048]{3,2,1,0:T(8,128)(2,1)}, f32[128,2048]{1,0:T(8,128)}, f32[8,2048]{1,0:T(8,128)}, bf16[4,1,128,2048]{3,2,1,0:T(8,128)(2,1)}, ...) custom-call(bf16[4,32,8,1024]{3,2,1,0:T(8,128)(2,1)} %bitcast.65, ...), custom_call_target="tpu_custom_call" | custom-call | tf_op jit(solution)/shard_map/pallas_call | solution.py:1326
  340.5 94.4 %shard_map.243 = (bf16[4,1,128,2048]{3,2,1,0:T(8,128)(2,1)}, f32[8,2048]{1,0:T(8,128)}, bf16[2,32,8,1024]{3,2,1,0:T(8,128)(2,1)}, bf16[2,1,2,16,8,512]{5,4,3,2,1...) custom-call(bf16[4,256,768]{2,1,0:T(8,128)(2,1)} %bitcast.73, ...), custom_call_target="tpu_custom_call" | custom-call | tf_op jit(solution)/shard_map/pallas_call | solution.py:1496
  434.8 12.7 %shard_map.244 = (bf16[512,2048]{1,0:T(8,128)(2,1)}, bf16[512,2048]{1,0:T(8,128)(2,1)}, f32[512,512]{1,0:T(8,128)}, f32[512,512]{1,0:T(8,128)}, f32[512,512]{1,0...) custom-call(f32[8,2048]{1,0:T(8,128)} %get-tuple-element.89.small, ...), custom_call_target="tpu_custom_call" | custom-call | tf_op jit(solution)/shard_map/pallas_call | solution.py:1558
  447.5 1.2 slice_bitcast_fusion
